TPU v7x, 768 devices: a whole 4x8x12 slice. The times are simulated.
768 devices in a mesh: src: 8 (over y), dst: 96 (over z, x, core).
Axes of the slice: x: 4, y: 8, z: 12, core: 2. Of those that a mesh axis runs over, the one named last changes fastest.
Arguments:
- node_feats: bfloat16 [12288, 256], P(('dst', 'src')), may hold values from -6 to 6
- cotangent: bfloat16 [12288, 256], P(('src', 'dst')), may hold values from -6 to 6
- edge_attr: bfloat16 [1179648, 128], P(('src', 'dst')), may hold values from -6 to 6
- src_ids: int32 [1179648], P(('src', 'dst')), may hold values from 0 to 127
- dst_rel: int32 [1179648], P(('src', 'dst')), may hold values from 0 to 127
- offsets: int32 [9216], P(('src', 'dst')), may hold values from 0 to 1408
- counts: int32 [9216], P(('src', 'dst')), may hold values from 32 to 128
- w_node: bfloat16 [256, 512], replicated, may hold values from -0.375 to 0.375
- w_edge: bfloat16 [128, 512], replicated, may hold values from -0.5 to 0.5
- bias: float32 [512], replicated, may hold values from -3 to 3
- w_out: bfloat16 [512, 256], replicated, may hold values from -0.03125 to 0.03125
Outputs:
- aggregated: bfloat16 [12288, 256], P(('src', 'dst'))
- node_grads: bfloat16 [12288, 256], P(('dst', 'src'))
- attr_grads: bfloat16 [1179648, 128], P(('src', 'dst'))
Inputs may be any that keep to these rules, and one draw needn't show every extreme that they name: `counts`: slots at or after a block's count carry no edge; their ids are arbitrary within range.
All inputs are finite; a program needn't handle non-finite values.
Results may differ from a plain program's by a relative error of at most 0.0049.
Values may be sent and summed in bfloat16 or wider, within the bound.
A program may use at most 32 MiB of HBM per device.

v0:
```python
import jax
import jax.numpy as jnp
from jax import lax
from jax.sharding import PartitionSpec as P


def first_layer(x_edges, edge_attr, w_node, w_edge, bias):
    return (
        jnp.dot(x_edges, w_node, preferred_element_type=jnp.float32)
        + jnp.dot(edge_attr, w_edge, preferred_element_type=jnp.float32)
        + bias
    )


def local(
    node_feats, cotangent, edge_attr, src_ids, dst_rel, offsets, counts, w_node, w_edge, bias, w_out
):
    edges = src_ids.shape[0]
    blocks = offsets.shape[0]
    width = edges // blocks
    owned = node_feats.shape[0]
    feat = node_feats.shape[1]
    dst_rows = owned * lax.axis_size("dst")
    slots = lax.broadcasted_iota(jnp.int32, (blocks, width), 1)
    valid_grid = slots < counts[:, None]
    rel_grid = dst_rel.reshape(blocks, width)
    window_iota = lax.broadcasted_iota(jnp.int32, (blocks, width, width), 2)
    dst_hot = ((rel_grid[:, :, None] == window_iota) & valid_grid[:, :, None]).astype(jnp.float32)
    group = lax.all_gather(node_feats, "src", axis=0, tiled=True)
    group_rows = group.shape[0]
    src_hot = (src_ids[:, None] == lax.broadcasted_iota(jnp.int32, (edges, group_rows), 1)).astype(
        jnp.bfloat16
    )
    x_edges = jnp.dot(src_hot, group, preferred_element_type=jnp.float32).astype(jnp.bfloat16)
    pre = first_layer(x_edges, edge_attr, w_node, w_edge, bias)
    hidden = jax.nn.silu(pre).astype(jnp.bfloat16)
    message = jnp.dot(hidden, w_out, preferred_element_type=jnp.float32)
    block_sums = jnp.einsum(
        "bjr,bjw->brw",
        dst_hot,
        message.reshape(blocks, width, feat),
        precision=lax.Precision.HIGHEST,
    )

    def add_block(index, total):
        start = offsets[index]
        current = lax.dynamic_slice_in_dim(total, start, width, 0)
        return lax.dynamic_update_slice_in_dim(total, current + block_sums[index], start, 0)

    partial_sums = lax.fori_loop(0, blocks, add_block, jnp.zeros((dst_rows, feat), jnp.float32))
    aggregated = lax.psum_scatter(partial_sums, "dst", scatter_dimension=0, tiled=True)
    gathered = lax.all_gather(cotangent, "dst", axis=0, tiled=True)
    windows = jax.vmap(lambda start: lax.dynamic_slice_in_dim(gathered, start, width, 0))(offsets)
    d_message = (
        jnp.einsum(
            "bjr,brw->bjw",
            dst_hot.astype(jnp.bfloat16),
            windows,
            preferred_element_type=jnp.float32,
        )
        .astype(jnp.bfloat16)
        .reshape(edges, feat)
    )
    d_hidden = jnp.dot(d_message, w_out.T, preferred_element_type=jnp.float32)
    sig = jax.nn.sigmoid(pre)
    d_pre = (d_hidden * sig * (1.0 + pre * (1.0 - sig))).astype(jnp.bfloat16)
    attr_grads = jnp.dot(d_pre, w_edge.T, preferred_element_type=jnp.float32).astype(jnp.bfloat16)
    d_source = jnp.dot(d_pre, w_node.T, preferred_element_type=jnp.float32)
    source_sums = jnp.dot(src_hot.astype(jnp.float32).T, d_source, precision=lax.Precision.HIGHEST)
    node_grads = lax.psum_scatter(source_sums, "src", scatter_dimension=0, tiled=True)
    return (aggregated.astype(jnp.bfloat16), node_grads.astype(jnp.bfloat16), attr_grads)


def solution(mesh):
    in_specs = (
        P(("dst", "src"), None),
        P(("src", "dst"), None),
        P(("src", "dst"), None),
        P(("src", "dst")),
        P(("src", "dst")),
        P(("src", "dst")),
        P(("src", "dst")),
        P(),
        P(),
        P(),
        P(),
    )
    out_specs = (P(("src", "dst"), None), P(("dst", "src"), None), P(("src", "dst"), None))
    return jax.shard_map(local, mesh=mesh, in_specs=in_specs, out_specs=out_specs, check_vma=False)
```

profile of v0, /device:TPU:16, one launch (start us, length us, event | category | flops | bytes accessed | tf_op | source)
XLA Modules:
  0.0 419.9 jit_solution(5803037181412009218)
XLA Ops:
  8.0 85.3 %all_gather.7 = bf16[1536,256]{1,0:T(8,128)(2,1)S(1)} all-gather(bf16[16,256]{1,0:T(8,128)(2,1)} %param.14), channel_id=1, replica_groups=mesh['src'=8,'dst'=96] {'dst'}, dimensions={0}, use_global_device_ids=true | all-gather | bytes 794624 | tf_op jit(solution)/shard_map/all_gather | solution.py:52
  94.0 15.3 %while.15 = (s32[]{:T(128)}, bf16[1536,256]{1,0:T(8,128)(2,1)S(1)}, s32[12,2]{0,1:T(2,128)S(1)}, bf16[12,128,256]{2,1,0:T(8,128)(2,1)S(1)}, s32[]{:T(128)}) while((s32[]{:T(128)}, bf16[1536,256]{1,0:T(8,128)(2,1)S(1)}, s32[12,2]{0,1:T(2,128)S(1)}, bf16[12,128,256]{2,1,0:T(8,128)(2,1)S(1)}, s32[]{:T(128)}) %tuple.46), condition=%wide.while_cond, body=%wide.while_body.sunk | while | flops 2 | bytes 131169 | solution.py:53
  109.3 27.7 %all_gather.6 = bf16[128,256]{1,0:T(8,128)(2,1)} all-gather(bf16[16,256]{1,0:T(8,128)(2,1)S(1)} %copy-done.11), channel_id=1, replica_groups=mesh['src'=8,'dst'=96] {'src'}, dimensions={0}, use_global_device_ids=true | all-gather | bytes 73728 | tf_op jit(solution)/shard_map/all_gather | solution.py:29
  137.0 1.6 convolution_convert_fusion.2
  138.6 1.8 fusion.4
  140.5 1.5 fusion.1
  142.1 1.4 fusion.2
  144.8 1.8 fusion.5
  146.7 2.8 fusion.3
  149.5 2.5 fusion.7
  152.7 53.9 %while.14 = (s32[]{:T(128)}, f32[1536,256]{1,0:T(8,128)S(1)}, s32[12]{0:T(128)S(1)}, f32[12,128,256]{2,1,0:T(8,128)}, s32[]{:T(128)}, /*index=5*/s32[]{:T(128)}, s32[]{:T(128)}) while((s32[]{:T(128)}, f32[1536,256]{1,0:T(8,128)S(1)}, s32[12]{0:T(128)S(1)}, f32[12,128,256]{2,1,0:T(8,128)}, s32[]{:T(128)}, /*index=5*/s32[]{:T(128)}, ...), condition=%wide.region_1.2_spmd, body=%wide.region_0.1_spmd.sunk | while | flops 32773 | bytes 655495 | solution.py:50
  156.1 1.0 dynamic_update_slice.8
  160.6 1.0 dynamic_update_slice.8
  164.2 0.9 bitcast_add_fusion.2
  165.1 1.0 dynamic_update_slice.8
  169.6 1.0 dynamic_update_slice.8
  174.1 1.0 dynamic_update_slice.8
  177.7 0.9 bitcast_add_fusion.2
  178.6 1.0 dynamic_update_slice.8
  183.1 1.0 dynamic_update_slice.8
  187.6 1.0 dynamic_update_slice.8
  191.1 0.9 bitcast_add_fusion.2
  192.1 1.0 dynamic_update_slice.8
  195.6 0.9 bitcast_add_fusion.2
  196.6 1.0 dynamic_update_slice.8
  201.0 1.0 dynamic_update_slice.8
  205.5 1.0 dynamic_update_slice.8
  206.6 1.2 copy-done.1
  208.5 2.2 convolution_convert_fusion.1
  210.8 1.3 convert_element_type.36
  212.1 199.7 %reduce-scatter.3.cloned.1.call-done = f32[16,256]{1,0:T(8,128)} async-done(((f32[1536,256]{1,0:T(8,128)}), f32[16,256]{1,0:T(8,128)}) %reduce-scatter.3.cloned.1.call-update) | async-done | bytes 16400 | tf_op jit(solution)/shard_map/reduce_scatter | solution.py:51
  411.7 1.3 convert_element_type.31
  (96 shorter events, 34.0 us)
Async XLA Ops:
  7.2 133.3 %copy-start = (bf16[1536,128]{1,0:T(8,128)(2,1)S(1)}, bf16[1536,128]{1,0:T(8,128)(2,1)}, u32[]{:S(2)}) copy-start(bf16[1536,128]{1,0:T(8,128)(2,1)} %param.15) | copy-start | bytes 1179652
  7.2 102.1 %copy-start.11 = (bf16[16,256]{1,0:T(8,128)(2,1)S(1)}, bf16[16,256]{1,0:T(8,128)(2,1)}, u32[]{:S(2)}) copy-start(bf16[16,256]{1,0:T(8,128)(2,1)} %param.13) | copy-start | bytes 24580
  7.2 129.8 %copy-start.8 = (s32[1536]{0:T(1024)S(1)}, s32[1536]{0:T(1024)}, u32[]{:S(2)}) copy-start(s32[1536]{0:T(1024)} %param.17) | copy-start | bytes 18436
  7.2 203.6 %reduce-scatter.5.cloned.1.call-start = ((), (), s32[]{:S(2)}) async-start(), calls=%async_computation.3 | async-start | bytes 147456 | tf_op jit(solution)/shard_map/reduce_scatter | solution.py:70
  8.0 129.0 %copy-start.9 = (pred[12,128]{1,0:T(8,128)(4,1)}, pred[12,128]{1,0:T(8,128)(4,1)S(1)}, u32[]{:S(2)}) copy-start(pred[12,128]{1,0:T(8,128)(4,1)S(1)} %iota_compare_fusion.5) | copy-start | bytes 4612
  8.0 130.6 %copy-start.7 = (s32[1536]{0:T(1024)S(1)}, s32[1536]{0:T(1024)}, u32[]{:S(2)}) copy-start(s32[1536]{0:T(1024)} %param.16) | copy-start | bytes 18436
  140.4 1.6 copy-start.6
  140.4 1.6 copy-start.12
  142.0 1.7 copy-start.4
  142.0 1.6 copy-start.5
  143.7 1.2 copy-start.2
  144.8 1.8 copy-start.13
  146.6 2.9 copy-start.10
  146.6 265.1 %reduce-scatter.3.cloned.1.call-start = ((), (), s32[]{:S(2)}) async-start(), calls=%async_computation.2 | async-start | bytes 1589248 | tf_op jit(solution)/shard_map/reduce_scatter | solution.py:51
  152.0 0.7 copy-start.14
  206.6 1.2 copy-start.1
  206.6 2.0 copy-start.3
Sparse Core Ops, SparseCore 0:
  146.7 34.1 reduce-scatter.4
  207.9 203.8 reduce-scatter.2
where the time goes:
time: 421 us; the launch traced here: 420 us
  waiting for transfers between devices  200 us (48%)
  blocking collectives  113 us (27%)
  local copies, waits for them, and re-layouts  37.5 us (9%)
  loops' own time  23.9 us (6%)
  matrix products  16.2 us (4%)
  other arithmetic  15.3 us (4%)
  between operations  14.2 us (3%)
    reduce_scatter x1, waiting for transfers between devices, local(): lax.psum_scatter(partial_sums, 'dst', scatter_dimension=0, tiled=True)  200 us
    all_gather x1, blocking collectives, local(): gathered = lax.all_gather(cotangent, 'dst', axis=0, tiled=True)  85.3 us
    all_gather x1, blocking collectives, local(): group = lax.all_gather(node_feats, 'src', axis=0, tiled=True)  27.7 us
    another operation x1, loops' own time, local(): lax.fori_loop(0, blocks, add_block, jnp.zeros((dst_rows, feat), jnp.float...  23.6 us
    gather x36, local copies, waits for them, and re-layouts  15.1 us
    dynamic_update_slice x12, local copies, waits for them, and re-layouts, add_block(): lax.dynamic_update_slice_in_dim(total, current + block_sums[index], start...  12 us
    add x12, other arithmetic, add_block(): current + block_sums[index]  11.2 us
  transfers between devices with their start and end apart: 2, of which 1 were waited for; matrix products, arithmetic and copies ran while one was open for 9% of the time, Pallas kernels for 0%

commit v1 on v0

v1 whole, which is shorter than its diff:
```python
import functools

import jax
import jax.numpy as jnp
from jax import lax
from jax.experimental import pallas as pl
from jax.experimental.pallas import tpu as pltpu
from jax.sharding import PartitionSpec as P

MESH = pl.DeviceIdType.MESH
X_CHIPS = 4
CORES = 2
WINDOW = 256
NT = (((1,), (1,)), ((), ()))


def split_bf16(value):
    high = value.astype(jnp.bfloat16)
    low = (value - high.astype(jnp.float32)).astype(jnp.bfloat16)
    return high, low


def kernel(
    dims,
    feats_in, cot_in, attr_in, src_in, rel_in, offsets, counts, wnode_in, wedge_in, bias_in, wout_in,
    agg_out, node_out, attr_out,
    group, cot, attr, src, rel, wnode, wedge, bias, wout,
    hot_src, hot_src_t, hot_dst, hot_win,
    proj, pre, msg, dpre, attr_grad,
    half_out, half_in, own, x_out, x_in, z_out, z_in, s_out, s_in, agg, node,
    load_sem, feat_send, feat_recv, cx_send, cx_recv, cz_send, cz_recv, cc_send, cc_recv,
    half_send, half_recv, x_send, x_recv, z_send, z_recv, s_send, s_recv, store_sem,
):
    n_src, n_x, n_z, rows = dims
    blocks, width = src.shape
    edges = blocks * width
    feat = group.shape[2]
    me_s = lax.axis_index("src")
    me_d = lax.axis_index("dst")
    me_c = lax.rem(me_d, CORES)
    me_x = lax.rem(lax.div(me_d, CORES), n_x)
    me_z = lax.div(me_d, CORES * n_x)
    slab = rows * n_z
    half = slab * n_x

    def dst_at(z, x, c):
        return (z * n_x + x) * CORES + c

    def y_peer(k):
        return (lax.rem(me_s + k, n_src), me_d)

    def x_peer(k):
        return (me_s, dst_at(me_z, lax.rem(me_x + k, n_x), me_c))

    def z_peer(k):
        return (me_s, dst_at(lax.rem(me_z + k, n_z), me_x, me_c))

    sibling = (me_s, dst_at(me_z, me_x, 1 - me_c))

    def remote(source, target, send, recv, device):
        return pltpu.make_async_remote_copy(
            src_ref=source, dst_ref=target, send_sem=send, recv_sem=recv,
            device_id=device, device_id_type=MESH,
        )

    def loop(first, last, step):
        def body(k, carry):
            step(k)
            return carry
        lax.fori_loop(first, last, body, 0)

    loads = [
        pltpu.make_async_copy(source, target, load_sem.at[i])
        for i, (source, target) in enumerate(
            (
                (src_in, src), (rel_in, rel), (attr_in, attr), (wedge_in, wedge), (bias_in, bias),
                (wnode_in, wnode), (wout_in, wout),
                (feats_in, group.at[me_s]), (cot_in, cot.at[me_z * n_x + me_x, me_c]),
            )
        )
    ]
    for load in loads:
        load.start()

    barrier = pltpu.get_barrier_semaphore()

    def greet(device):
        pl.semaphore_signal(barrier, inc=1, device_id=device, device_id_type=MESH)

    loop(1, n_src, lambda k: greet(y_peer(k)))
    loop(1, n_x, lambda k: greet(x_peer(k)))
    loop(1, n_z, lambda k: greet(z_peer(k)))
    greet(sibling)
    pl.semaphore_wait(barrier, n_src + n_x + n_z - 2)

    def feat_copy(k):
        return remote(feats_in, group.at[me_s], feat_send.at[k], feat_recv.at[k], y_peer(k))

    def cx_copy(k):
        return remote(
            cot_in, cot.at[me_z * n_x + me_x, me_c], cx_send.at[k], cx_recv.at[k], x_peer(k)
        )

    loop(1, n_src, lambda k: feat_copy(k).start())
    loop(1, n_x, lambda k: cx_copy(k).start())

    def own_slab(z):
        return cot.at[pl.ds(z * n_x, n_x), me_c]

    def cz_copy(k):
        return remote(own_slab(me_z), own_slab(me_z), cz_send.at[k], cz_recv.at[k], z_peer(k))

    def cc_copy(k):
        z = lax.rem(me_z + n_z - k, n_z)
        return remote(own_slab(z), own_slab(z), cc_send.at[k], cc_recv.at[k], sibling)

    loads[0].wait()
    loads[1].wait()
    lane = lax.broadcasted_iota(jnp.int32, (width, width), 1)
    sub = lax.broadcasted_iota(jnp.int32, (width, width), 0)
    tall = lax.broadcasted_iota(jnp.int32, (CORES * half, width), 0)
    one_lane = lax.broadcasted_iota(jnp.int32, (1, width), 1)

    def hot(mask):
        return jnp.where(mask, 1.0, 0.0).astype(jnp.bfloat16)

    def mark(b):
        at = pl.multiple_of(b * width, width)
        here = pl.ds(at, width)
        ids = src[pl.ds(b, 1), :]
        picked = hot(jnp.broadcast_to(ids, (width, width)).T == lane)
        hot_src[here, 0:width] = picked
        hot_src[here, width : 2 * width] = picked
        owner = lax.rem((ids >> 4) + (n_src - me_s), n_src)
        hot_src_t[:, here] = hot(sub[: n_src * rows] == owner * rows + (ids & (rows - 1)))
        valid = one_lane < counts[b]
        start = offsets[b]
        target = rel[pl.ds(b, 1), :] + start
        peer = target >> 4
        core = lax.rem(peer + me_c, CORES)
        x = lax.rem((peer >> 1) + (n_x - me_x), n_x)
        z = lax.rem(lax.div(peer, CORES * n_x) + (n_z - me_z), n_z)
        place = ((core * n_x + x) * n_z + z) * rows + (target & (rows - 1))
        hot_dst[:, here] = hot(tall == jnp.where(valid, place, -1))
        base = jnp.minimum(start >> 5, cot.shape[0] - WINDOW // (CORES * rows)) * (CORES * rows)
        inside = jnp.broadcast_to(jnp.where(valid, target - base, -1), (width, width)).T
        hot_win[here, 0:width] = hot(inside == lane)
        hot_win[here, width : 2 * width] = hot(inside == lane + width)

    loop(0, blocks, mark)

    for i in (2, 3, 4):
        loads[i].wait()
    tile = min(256, edges)

    def attr_part(i):
        here = pl.ds(pl.multiple_of(i * tile, tile), tile)
        pre[here, :] = (
            jnp.dot(attr[here, :], wedge[...], preferred_element_type=jnp.float32) + bias[...]
        )

    loop(0, edges // tile, attr_part)

    loads[8].wait()
    loop(1, n_x, lambda k: cx_copy(k).wait_recv())
    loop(1, n_z, lambda k: cz_copy(k).start())
    cc_copy(0).start()

    loads[5].wait()
    loads[6].wait()
    loads[7].wait()
    loop(1, n_src, lambda k: feat_copy(k).wait_recv())
    high, low = split_bf16(
        jnp.dot(
            group[...].reshape(n_src * rows, feat), wnode[...], preferred_element_type=jnp.float32
        )
    )
    if n_src * rows < width:
        proj[...] = jnp.zeros_like(proj)
    proj[0 : n_src * rows, :] = high
    proj[width : width + n_src * rows, :] = low

    def forward(i):
        here = pl.ds(pl.multiple_of(i * tile, tile), tile)
        value = pre[here, :] + jnp.dot(
            hot_src[here, :], proj[...], preferred_element_type=jnp.float32
        )
        sig = 0.5 * jnp.tanh(0.5 * value) + 0.5
        hidden = (value * sig).astype(jnp.bfloat16)
        pre[here, :] = sig * (1.0 + value * (1.0 - sig))
        msg[here, :] = jnp.dot(hidden, wout[...], preferred_element_type=jnp.float32).astype(
            jnp.bfloat16
        )

    loop(0, edges // tile, forward)

    def half_copy(k):
        part = pl.ds(k * slab, slab)
        return remote(
            half_out.at[part], half_in.at[part], half_send.at[k], half_recv.at[k], sibling
        )

    def x_copy(k):
        return remote(
            x_out.at[k - 1], x_in.at[k - 1], x_send.at[k - 1], x_recv.at[k - 1], x_peer(k)
        )

    order = tuple(range(1, n_x)) + (0,)
    for k in order:
        half_out[k * slab : (k + 1) * slab, :] = jnp.dot(
            hot_dst[half + k * slab : half + (k + 1) * slab, :],
            msg[...],
            preferred_element_type=jnp.float32,
        )
        half_copy(k).start()
    for k in order:
        total = jnp.dot(
            hot_dst[k * slab : (k + 1) * slab, :], msg[...], preferred_element_type=jnp.float32
        )
        half_copy(k).wait_recv()
        total = total + half_in[k * slab : (k + 1) * slab, :]
        if k:
            x_out[k - 1] = total.astype(jnp.bfloat16)
            x_copy(k).start()
        else:
            own[...] = total

    def z_copy(k):
        return remote(
            z_out.at[k - 1], z_in.at[k - 1], z_send.at[k - 1], z_recv.at[k - 1], z_peer(k)
        )

    for k in range(1, n_x):
        x_copy(k).wait_recv()
    summed = own[...]
    for k in range(1, n_x):
        summed = summed + x_in[k - 1].astype(jnp.float32)
    own[...] = summed
    z_out[...] = summed[rows:].astype(jnp.bfloat16).reshape(n_z - 1, rows, feat)
    loop(1, n_z, lambda k: z_copy(k).start())

    def pass_on(k):
        cz_copy(k).wait_recv()
        cc_copy(k).start()

    loop(1, n_z, pass_on)
    loop(0, n_z, lambda k: cc_copy(k).wait_recv())

    def backward(b):
        here = pl.ds(pl.multiple_of(b * width, width), width)
        first = jnp.minimum(offsets[b] >> 5, cot.shape[0] - WINDOW // (CORES * rows))
        window = cot[pl.ds(first, WINDOW // (CORES * rows))].reshape(WINDOW, feat)
        d_message = jnp.dot(
            hot_win[here, :], window, preferred_element_type=jnp.float32
        ).astype(jnp.bfloat16)
        d_hidden = lax.dot_general(d_message, wout[...], NT, preferred_element_type=jnp.float32)
        d_pre = (d_hidden * pre[here, :]).astype(jnp.bfloat16)
        dpre[here, :] = d_pre
        attr_grad[here, :] = lax.dot_general(
            d_pre, wedge[...], NT, preferred_element_type=jnp.float32
        ).astype(jnp.bfloat16)

    loop(0, blocks, backward)
    attr_store = pltpu.make_async_copy(attr_grad, attr_out, store_sem.at[0])
    attr_store.start()
    high, low = split_bf16(
        jnp.dot(hot_src_t[...], dpre[...], preferred_element_type=jnp.float32)
    )
    sums = lax.dot_general(
        high, wnode[...], NT, preferred_element_type=jnp.float32
    ) + lax.dot_general(low, wnode[...], NT, preferred_element_type=jnp.float32)
    s_out[...] = sums.reshape(n_src, rows, feat)

    def s_copy(k):
        return remote(s_out.at[k], s_in.at[k - 1], s_send.at[k - 1], s_recv.at[k - 1], y_peer(k))

    loop(1, n_src, lambda k: s_copy(k).start())

    loop(1, n_z, lambda k: z_copy(k).wait_recv())
    agg[...] = (own[0:rows, :] + jnp.sum(z_in[...].astype(jnp.float32), axis=0)).astype(jnp.bfloat16)
    agg_store = pltpu.make_async_copy(agg, agg_out, store_sem.at[1])
    agg_store.start()
    loop(1, n_src, lambda k: s_copy(k).wait_recv())
    node[...] = (s_out[0] + jnp.sum(s_in[...], axis=0)).astype(jnp.bfloat16)
    node_store = pltpu.make_async_copy(node, node_out, store_sem.at[2])
    node_store.start()

    loop(1, n_src, lambda k: feat_copy(k).wait_send())
    loop(1, n_x, lambda k: cx_copy(k).wait_send())
    loop(1, n_z, lambda k: cz_copy(k).wait_send())
    loop(0, n_z, lambda k: cc_copy(k).wait_send())
    for k in range(n_x):
        half_copy(k).wait_send()
    for k in range(1, n_x):
        x_copy(k).wait_send()
    loop(1, n_z, lambda k: z_copy(k).wait_send())
    loop(1, n_src, lambda k: s_copy(k).wait_send())
    attr_store.wait()
    agg_store.wait()
    node_store.wait()


def local(
    n_src, n_x, n_z,
    node_feats, cotangent, edge_attr, src_ids, dst_rel, offsets, counts, w_node, w_edge, bias, w_out,
):
    rows, feat = node_feats.shape
    edges, attr_width = edge_attr.shape
    blocks = offsets.shape[0]
    width = edges // blocks
    hidden = w_node.shape[1]
    slab = rows * n_z
    half = slab * n_x
    f32, bf16 = jnp.float32, jnp.bfloat16
    vmem, dma = pltpu.VMEM, pltpu.SemaphoreType.DMA
    anywhere = pl.BlockSpec(memory_space=pl.ANY)
    scalars = pl.BlockSpec(memory_space=pltpu.SMEM)
    return pl.pallas_call(
        functools.partial(kernel, (n_src, n_x, n_z, rows)),
        out_shape=(
            jax.ShapeDtypeStruct((rows, feat), bf16),
            jax.ShapeDtypeStruct((rows, feat), bf16),
            jax.ShapeDtypeStruct((edges, attr_width), bf16),
        ),
        in_specs=[anywhere] * 5 + [scalars] * 2 + [anywhere] * 4,
        out_specs=(anywhere,) * 3,
        scratch_shapes=[
            vmem((n_src, rows, feat), bf16),
            vmem((n_z * n_x, CORES, rows, feat), bf16),
            vmem((edges, attr_width), bf16),
            vmem((blocks, width), jnp.int32),
            vmem((blocks, width), jnp.int32),
            vmem(w_node.shape, bf16),
            vmem(w_edge.shape, bf16),
            vmem((1, hidden), f32),
            vmem(w_out.shape, bf16),
            vmem((edges, 2 * width), bf16),
            vmem((n_src * rows, edges), bf16),
            vmem((CORES * half, edges), bf16),
            vmem((edges, WINDOW), bf16),
            vmem((2 * width, hidden), bf16),
            vmem((edges, hidden), f32),
            vmem((edges, feat), bf16),
            vmem((edges, hidden), bf16),
            vmem((edges, attr_width), bf16),
            vmem((half, feat), f32),
            vmem((half, feat), f32),
            vmem((slab, feat), f32),
            vmem((n_x - 1, slab, feat), bf16),
            vmem((n_x - 1, slab, feat), bf16),
            vmem((n_z - 1, rows, feat), bf16),
            vmem((n_z - 1, rows, feat), bf16),
            vmem((n_src, rows, feat), f32),
            vmem((n_src - 1, rows, feat), f32),
            vmem((rows, feat), bf16),
            vmem((rows, feat), bf16),
            dma((9,)),
            dma((n_src,)),
            dma((n_src,)),
            dma((n_x,)),
            dma((n_x,)),
            dma((n_z,)),
            dma((n_z,)),
            dma((n_z,)),
            dma((n_z,)),
            dma((n_x,)),
            dma((n_x,)),
            dma((n_x - 1,)),
            dma((n_x - 1,)),
            dma((n_z - 1,)),
            dma((n_z - 1,)),
            dma((n_src - 1,)),
            dma((n_src - 1,)),
            dma((3,)),
        ],
        compiler_params=pltpu.CompilerParams(
            collective_id=0, has_side_effects=True, vmem_limit_bytes=48 * 1024 * 1024
        ),
    )(
        node_feats, cotangent, edge_attr,
        src_ids.reshape(blocks, width), dst_rel.reshape(blocks, width), offsets, counts,
        w_node, w_edge, bias.reshape(1, hidden), w_out,
    )


def build(mesh, n_x):
    n_src, n_dst = mesh.shape["src"], mesh.shape["dst"]
    in_specs = (
        P(("dst", "src"), None),
        P(("src", "dst"), None),
        P(("src", "dst"), None),
        P(("src", "dst")),
        P(("src", "dst")),
        P(("src", "dst")),
        P(("src", "dst")),
        P(),
        P(),
        P(),
        P(),
    )
    out_specs = (P(("src", "dst"), None), P(("dst", "src"), None), P(("src", "dst"), None))
    return jax.shard_map(
        functools.partial(local, n_src, n_x, n_dst // (n_x * CORES)),
        mesh=mesh, in_specs=in_specs, out_specs=out_specs, check_vma=False,
    )


def solution(mesh):
    return build(mesh, X_CHIPS)
```

time: 421 us -> 64.8 us (0.15)
  the two profiles are of different devices: /device:TPU:16 before, /device:TPU:1 now
where the time goes in v1:
time: 64.8 us; the launch traced here: 64.3 us
  Pallas kernels  54.4 us (84%)
  local copies, waits for them, and re-layouts  9.19 us (14%)
  between operations  0.68 us (1%)
    pallas_call x1, Pallas kernels, local(): pl.pallas_call(functools.partial(kernel, (n_src, n_x, n_z, rows)), out_sh...  54.4 us
    unnamed x25, local copies, waits for them, and re-layouts  9.19 us

profile of v1, /device:TPU:1, one launch (start us, length us, event | category | flops | bytes accessed | tf_op | source)
XLA Modules:
  0.0 64.3 jit_solution(4545064027854057109)
XLA Ops:
  0.6 0.0 copy-start.8
  0.6 0.0 copy-start.9
  0.7 0.0 copy-start.10
  0.7 0.7 %copy-done.8 = f32[512]{0:T(512)S(1)} copy-done((f32[512]{0:T(512)S(1)}, f32[512]{0:T(512)}, u32[]{:S(2)}) %copy-start.8) | copy-done | bytes 2072
  1.3 0.0 copy-done.9
  1.3 0.0 copy-done.10
  1.3 0.0 copy-start
  1.3 1.0 %copy-done = bf16[1536,128]{1,0:T(8,128)(2,1)S(1)} copy-done((bf16[1536,128]{1,0:T(8,128)(2,1)S(1)}, bf16[1536,128]{1,0:T(8,128)(2,1)}, u32[]{:S(2)}) %copy-start) | copy-done | bytes 393240
  2.3 0.0 copy-start.1
  2.3 0.9 %copy-done.1 = bf16[256,512]{1,0:T(8,128)(2,1)S(1)} copy-done((bf16[256,512]{1,0:T(8,128)(2,1)S(1)}, bf16[256,512]{1,0:T(8,128)(2,1)}, u32[]{:S(2)}) %copy-start.1) | copy-done | bytes 262168
  3.3 0.0 copy-start.2
  3.3 0.9 %copy-done.2 = bf16[512,256]{1,0:T(8,128)(2,1)S(1)} copy-done((bf16[512,256]{1,0:T(8,128)(2,1)S(1)}, bf16[512,256]{1,0:T(8,128)(2,1)}, u32[]{:S(2)}) %copy-start.2) | copy-done | bytes 262168
  4.2 0.0 copy-start.3
  4.2 0.9 %copy-done.3 = bf16[128,512]{1,0:T(8,128)(2,1)S(1)} copy-done((bf16[128,512]{1,0:T(8,128)(2,1)S(1)}, bf16[128,512]{1,0:T(8,128)(2,1)}, u32[]{:S(2)}) %copy-start.3) | copy-done | bytes 131096
  5.1 0.0 copy-start.4
  5.1 0.7 %copy-done.4 = bf16[16,256]{1,0:T(8,128)(2,1)S(1)} copy-done((bf16[16,256]{1,0:T(8,128)(2,1)S(1)}, bf16[16,256]{1,0:T(8,128)(2,1)}, u32[]{:S(2)}) %copy-start.4) | copy-done | bytes 8216
  5.8 0.0 copy-start.5
  5.8 0.7 %copy-done.5 = bf16[16,256]{1,0:T(8,128)(2,1)S(1)} copy-done((bf16[16,256]{1,0:T(8,128)(2,1)S(1)}, bf16[16,256]{1,0:T(8,128)(2,1)}, u32[]{:S(2)}) %copy-start.5) | copy-done | bytes 8216
  6.5 0.0 copy-start.6
  6.5 0.7 %copy-done.6 = s32[1536]{0:T(1024)S(1)} copy-done((s32[1536]{0:T(1024)S(1)}, s32[1536]{0:T(1024)}, u32[]{:S(2)}) %copy-start.6) | copy-done | bytes 6168
  7.2 0.0 copy-start.7
  7.2 0.7 %copy-done.7 = s32[1536]{0:T(1024)S(1)} copy-done((s32[1536]{0:T(1024)S(1)}, s32[1536]{0:T(1024)}, u32[]{:S(2)}) %copy-start.7) | copy-done | bytes 6168
  7.9 54.4 %shard_map.130 = (bf16[16,256]{1,0:T(8,128)(2,1)S(1)}, bf16[16,256]{1,0:T(8,128)(2,1)S(1)}, bf16[1536,128]{1,0:T(8,128)(2,1)S(1)}) custom-call(bf16[16,256]{1,0:T(8,128)(2,1)S(1)} %copy-done.4, bf16[16,256]{1,0:T(8,128)(2,1)S(1)} %copy-done.5, bf16[1536,128]{1,0:T(8,128)(2,1)S(1)} %copy-done, s32[12,128]{1,0:T(8,128)S(1)} %bitcast.3, s32[12,128]{1,0:T(8,128)S(1)} %bitcast.4, ...), custom_call_target="tpu_custom_call" | custom-call | tf_op jit(solution)/shard_map/pallas_call | solution.py:318
  62.4 0.6 copy.17
  63.0 0.6 copy.18
  63.6 0.7 %copy.19 = bf16[1536,128]{1,0:T(8,128)(2,1)} copy(bf16[1536,128]{1,0:T(8,128)(2,1)S(1)} %get-tuple-element.8) | data formatting | bytes 786432
Async XLA Ops:
  0.6 0.7 %copy-start.8 = (f32[512]{0:T(512)S(1)}, f32[512]{0:T(512)}, u32[]{:S(2)}) copy-start(f32[512]{0:T(512)} %param.20) | copy-start | bytes 6148
  0.6 0.7 %copy-start.9 = (s32[12]{0:T(128)S(1)}, s32[12]{0:T(128)}, u32[]{:S(2)}) copy-start(s32[12]{0:T(128)} %offsets.1) | copy-start | bytes 148
  0.7 0.7 %copy-start.10 = (s32[12]{0:T(128)S(1)}, s32[12]{0:T(128)}, u32[]{:S(2)}) copy-start(s32[12]{0:T(128)} %counts.1) | copy-start | bytes 148
  1.3 1.0 %copy-start = (bf16[1536,128]{1,0:T(8,128)(2,1)S(1)}, bf16[1536,128]{1,0:T(8,128)(2,1)}, u32[]{:S(2)}) copy-start(bf16[1536,128]{1,0:T(8,128)(2,1)} %attr_in.1) | copy-start | bytes 1179652
  2.3 0.9 %copy-start.1 = (bf16[256,512]{1,0:T(8,128)(2,1)S(1)}, bf16[256,512]{1,0:T(8,128)(2,1)}, u32[]{:S(2)}) copy-start(bf16[256,512]{1,0:T(8,128)(2,1)} %wnode_in.1) | copy-start | bytes 786436
  3.3 0.9 %copy-start.2 = (bf16[512,256]{1,0:T(8,128)(2,1)S(1)}, bf16[512,256]{1,0:T(8,128)(2,1)}, u32[]{:S(2)}) copy-start(bf16[512,256]{1,0:T(8,128)(2,1)} %wout_in.1) | copy-start | bytes 786436
  4.2 0.9 %copy-start.3 = (bf16[128,512]{1,0:T(8,128)(2,1)S(1)}, bf16[128,512]{1,0:T(8,128)(2,1)}, u32[]{:S(2)}) copy-start(bf16[128,512]{1,0:T(8,128)(2,1)} %wedge_in.1) | copy-start | bytes 393220
  5.1 0.7 %copy-start.4 = (bf16[16,256]{1,0:T(8,128)(2,1)S(1)}, bf16[16,256]{1,0:T(8,128)(2,1)}, u32[]{:S(2)}) copy-start(bf16[16,256]{1,0:T(8,128)(2,1)} %feats_in.1) | copy-start | bytes 24580
  5.8 0.7 %copy-start.5 = (bf16[16,256]{1,0:T(8,128)(2,1)S(1)}, bf16[16,256]{1,0:T(8,128)(2,1)}, u32[]{:S(2)}) copy-start(bf16[16,256]{1,0:T(8,128)(2,1)} %cot_in.1) | copy-start | bytes 24580
  6.5 0.7 %copy-start.6 = (s32[1536]{0:T(1024)S(1)}, s32[1536]{0:T(1024)}, u32[]{:S(2)}) copy-start(s32[1536]{0:T(1024)} %param.14) | copy-start | bytes 18436
  7.2 0.7 %copy-start.7 = (s32[1536]{0:T(1024)S(1)}, s32[1536]{0:T(1024)}, u32[]{:S(2)}) copy-start(s32[1536]{0:T(1024)} %param.15) | copy-start | bytes 18436

commit v2 on v0

v2 whole, which is shorter than its diff:
```python
import functools

import jax
import jax.numpy as jnp
from jax import lax
from jax.experimental import pallas as pl
from jax.experimental.pallas import tpu as pltpu
from jax.sharding import PartitionSpec as P

MESH = pl.DeviceIdType.MESH
X_CHIPS = 4
CORES = 2
WINDOW = 256
NT = (((1,), (1,)), ((), ()))


def split_bf16(value):
    high = value.astype(jnp.bfloat16)
    low = (value - high.astype(jnp.float32)).astype(jnp.bfloat16)
    return high, low


def loop(first, last, step, unroll=1):
    def body(k, carry):
        step(k)
        return carry

    lax.fori_loop(first, last, body, 0, unroll=unroll)


def far_first(size, step, first=0, last=None):
    def body(i):
        step(size // 2 + (1 - 2 * lax.rem(i, 2)) * lax.div(i + 1, 2))

    loop(first, size - 1 if last is None else last, body)


def kernel(
    dims,
    feats_in, cot_in, attr_in, src_in, rel_in, offsets_in, counts_in, wnode_in, wedge_in, bias_in,
    wout_in,
    agg_out, node_out, attr_out,
    offsets, counts, group, cot, attr, src, rel, wnode, wedge, bias, wout,
    hot_src, hot_src_t, hot_dst, hot_win,
    proj, pre, msg, dpre, attr_grad,
    half_out, half_in, kept, own, far, x_out, x_in, b_out, b_in, far_out, far_in, z_out, z_in, s_out, s_in,
    agg, node,
    load_sem, half_recv, store_sem,
    feat_send, feat_recv, cot_send, cot_recv, cz_send, cz_recv, relay_send, relay_recv, cc_send, cc_recv, half_send,
    x_send, x_recv, b_send, b_recv, far_send, far_recv, z_send, z_recv, s_send, s_recv,
):
    n_src, n_x, n_z, rows = dims
    blocks, width = src.shape
    edges = blocks * width
    feat = group.shape[2]
    me_s = lax.axis_index("src")
    me_d = lax.axis_index("dst")
    me_c = lax.rem(me_d, CORES)
    me_x = lax.rem(lax.div(me_d, CORES), n_x)
    me_z = lax.div(me_d, CORES * n_x)
    slab = rows * n_z
    half = slab * n_x
    across = n_x // 2

    def dst_at(z, x, c):
        return (z * n_x + x) * CORES + c

    def y_peer(k):
        return (lax.rem(me_s + k, n_src), me_d)

    def peer(z, x):
        return (
            me_s, dst_at(lax.rem(me_z + z + n_z, n_z), lax.rem(me_x + x + n_x, n_x), me_c),
        )

    sibling = (me_s, dst_at(me_z, me_x, 1 - me_c))

    def remote(source, target, send, recv, device):
        return pltpu.make_async_remote_copy(
            src_ref=source, dst_ref=target, send_sem=send.at[0], recv_sem=recv,
            device_id=device, device_id_type=MESH,
        )

    def all_of(ref, send, recv):
        return remote(ref, ref, send, recv.at[0], sibling)


    with jax.named_scope("load"):
        loads = [
            pltpu.make_async_copy(source, target, load_sem.at[i])
            for i, (source, target) in enumerate(
                (
                    (feats_in, group.at[me_s]), (cot_in, cot.at[me_z * n_x + me_x, me_c]),
                    (src_in, src), (rel_in, rel), (offsets_in, offsets), (counts_in, counts),
                    (attr_in, attr), (wedge_in, wedge), (bias_in, bias),
                    (wnode_in, wnode), (wout_in, wout),
                )
            )
        ]
        for load in loads:
            load.start()

    with jax.named_scope("barrier"):
        barrier = pltpu.get_barrier_semaphore()

        def greet(device):
            pl.semaphore_signal(barrier, inc=1, device_id=device, device_id_type=MESH)

        far_first(n_src, lambda k: greet(y_peer(k)))
        far_first(n_z, lambda k: greet(peer(k, 0)))
        for k in range(1, n_x):
            greet(peer(0, k))
        greet(sibling)
        loads[0].wait()
        loads[1].wait()
        pl.semaphore_wait(barrier, (n_src - 1) + (n_z - 1) + (n_x - 1) + 1)

    with jax.named_scope("first_sends"):
        mine = group.at[me_s]
        far_first(
            n_src, lambda k: remote(mine, mine, feat_send, feat_recv.at[0], y_peer(k)).start()
        )

        def cot_at(z, x):
            return cot.at[z * n_x + lax.rem(me_x + x + n_x, n_x), me_c]

        def send_cot(z, x, send, recv, device):
            remote(cot_at(z, x), cot_at(z, x), send, recv.at[0], device).start()

        far_first(n_z, lambda k: send_cot(me_z, 0, cot_send, cot_recv, peer(k, 0)))

    with jax.named_scope("marks"):
        for i in (2, 3, 4, 5):
            loads[i].wait()
        lane = lax.broadcasted_iota(jnp.int32, (width, width), 1)
        sub = lax.broadcasted_iota(jnp.int32, (width, width), 0)
        tall = lax.broadcasted_iota(jnp.int32, (CORES * half, width), 0)
        one_lane = lax.broadcasted_iota(jnp.int32, (1, width), 1)
        last_window = cot.shape[0] - WINDOW // (CORES * rows)

        def hot(mask):
            return jnp.where(mask, 1.0, 0.0).astype(jnp.bfloat16)

        def mark(b):
            here = pl.ds(pl.multiple_of(b * width, width), width)
            ids = src[pl.ds(b, 1), :]
            picked = hot(jnp.broadcast_to(ids, (width, width)).T == lane)
            hot_src[here, 0:width] = picked
            hot_src[here, width : 2 * width] = picked
            owner = lax.rem((ids >> 4) + (n_src - me_s), n_src)
            hot_src_t[:, here] = hot(sub[: n_src * rows] == owner * rows + (ids & (rows - 1)))
            valid = one_lane < counts[b]
            start = offsets[b]
            target = rel[pl.ds(b, 1), :] + start
            owner = target >> 4
            core = lax.rem(owner + me_c, CORES)
            x = lax.rem((owner >> 1) + (n_x - me_x), n_x)
            z = lax.rem(lax.div(owner, CORES * n_x) + (n_z - me_z), n_z)
            place = ((core * n_x + x) * n_z + z) * rows + (target & (rows - 1))
            hot_dst[:, here] = hot(tall == jnp.where(valid, place, -1))
            base = jnp.minimum(start >> 5, last_window) * (CORES * rows)
            inside = jnp.broadcast_to(jnp.where(valid, target - base, -1), (width, width)).T
            hot_win[here, 0:width] = hot(inside == lane)
            hot_win[here, width : 2 * width] = hot(inside == lane + width)

        loop(0, blocks, mark)

    with jax.named_scope("attr_part"):
        for i in (6, 7, 8):
            loads[i].wait()
        tile = min(256, edges)

        def attr_part(i):
            here = pl.ds(pl.multiple_of(i * tile, tile), tile)
            pre[here, :] = (
                jnp.dot(attr[here, :], wedge[...], preferred_element_type=jnp.float32) + bias[...]
            )

        loop(0, edges // tile, attr_part, True)

    with jax.named_scope("feats_wait"):
        loads[9].wait()
        loads[10].wait()
        all_of(group.at[pl.ds(0, n_src - 1)], feat_send, feat_recv).wait_recv()

    with jax.named_scope("forward"):
        high, low = split_bf16(
            jnp.dot(
                group[...].reshape(n_src * rows, feat), wnode[...], preferred_element_type=jnp.float32
            )
        )
        if n_src * rows < width:
            proj[...] = jnp.zeros_like(proj)
        proj[0 : n_src * rows, :] = high
        proj[width : width + n_src * rows, :] = low

        def forward(i):
            here = pl.ds(pl.multiple_of(i * tile, tile), tile)
            value = pre[here, :] + jnp.dot(
                hot_src[here, :], proj[...], preferred_element_type=jnp.float32
            )
            sig = 0.5 * jnp.tanh(0.5 * value) + 0.5
            hidden = (value * sig).astype(jnp.bfloat16)
            pre[here, :] = sig * (1.0 + value * (1.0 - sig))
            msg[here, :] = jnp.dot(hidden, wout[...], preferred_element_type=jnp.float32).astype(
                jnp.bfloat16
            )

        loop(0, edges // tile, forward, True)

    with jax.named_scope("sums"):
        order = (across,) + tuple(k for k in range(1, n_x) if k != across) + (0,)

        def half_copy(k):
            part = pl.ds(k * slab, slab)
            return remote(half_out.at[part], half_in.at[part], half_send, half_recv.at[k], sibling)

        half_out[...] = jnp.dot(
            hot_dst[half : 2 * half, :], msg[...], preferred_element_type=jnp.float32
        ).astype(jnp.bfloat16)
        for k in order:
            half_copy(k).start()

    with jax.named_scope("cot_second"):
        all_of(cot.at[pl.ds(0, n_z - 1), 0], cot_send, cot_recv).wait_recv()

        def second(z):
            send_cot(z, 0, cz_send, cz_recv, peer(0, 1))
            send_cot(z, 0, cz_send, cz_recv, peer(0, -1))

        loop(0, n_z, second)
        loop(0, n_z, lambda z: send_cot(z, 0, cc_send, cc_recv, sibling))

    with jax.named_scope("sums_rest"):
        kept[...] = jnp.dot(hot_dst[0:half, :], msg[...], preferred_element_type=jnp.float32)
        slot = 0
        for k in order:
            part = slice(k * slab, (k + 1) * slab)
            half_copy(k).wait_recv()
            total = kept[part, :] + half_in[part, :].astype(jnp.float32)
            if k == across:
                far[...] = total[:rows]
                b_out[...] = total[rows:].astype(jnp.bfloat16).reshape(n_z - 1, rows, feat)
                far_first(
                    n_z,
                    lambda z: remote(
                        b_out.at[z - 1], b_in.at[z - 1], b_send, b_recv.at[0], peer(z, 0)
                    ).start(),
                )
            elif k:
                x_out[slot] = total.astype(jnp.bfloat16)
                remote(x_out.at[slot], x_in.at[slot], x_send, x_recv.at[0], peer(0, k)).start()
                slot += 1
            else:
                own[...] = total

    with jax.named_scope("cot_third"):
        all_of(cot.at[pl.ds(0, 2 * n_z), 0], cz_send, cz_recv).wait_recv()
        loop(0, n_z // 2, lambda z: send_cot(z, -1, relay_send, relay_recv, peer(0, 1)))
        loop(n_z // 2, n_z, lambda z: send_cot(z, 1, relay_send, relay_recv, peer(0, -1)))

        def pass_beside(z):
            send_cot(z, -1, cc_send, cc_recv, sibling)
            send_cot(z, 1, cc_send, cc_recv, sibling)

        loop(0, n_z, pass_beside)

    def backward(b):
        here = pl.ds(pl.multiple_of(b * width, width), width)
        first = jnp.minimum(offsets[b] >> 5, last_window)
        window = cot[pl.ds(first, WINDOW // (CORES * rows))].reshape(WINDOW, feat)
        d_message = jnp.dot(
            hot_win[here, :], window, preferred_element_type=jnp.float32
        ).astype(jnp.bfloat16)
        d_hidden = lax.dot_general(d_message, wout[...], NT, preferred_element_type=jnp.float32)
        d_pre = (d_hidden * pre[here, :]).astype(jnp.bfloat16)
        dpre[here, :] = d_pre
        attr_grad[here, :] = lax.dot_general(
            d_pre, wedge[...], NT, preferred_element_type=jnp.float32
        ).astype(jnp.bfloat16)

    with jax.named_scope("sums_x"):
        if n_x > 2:
            all_of(x_in, x_send, x_recv).wait_recv()
        summed = own[...]
        for k in range(n_x - 2):
            summed = summed + x_in[k].astype(jnp.float32)
        own[...] = summed
        z_out[...] = summed[rows:].astype(jnp.bfloat16).reshape(n_z - 1, rows, feat)
        far_first(
            n_z,
            lambda z: remote(
                z_out.at[z - 1], z_in.at[z - 1], z_send, z_recv.at[0], peer(z, 0)
            ).start(),
        )

    with jax.named_scope("cot_rest"):
        all_of(cot.at[pl.ds(0, n_z), 0], relay_send, relay_recv).wait_recv()
        loop(0, n_z, lambda z: send_cot(z, across, cc_send, cc_recv, sibling))

    with jax.named_scope("cot_last"):
        all_of(cot.at[:, 0], cc_send, cc_recv).wait_recv()

    with jax.named_scope("sums_far"):
        all_of(b_in, b_send, b_recv).wait_recv()
        far_out[...] = (far[...] + jnp.sum(b_in[...].astype(jnp.float32), axis=0)).astype(jnp.bfloat16)
        far_copy = remote(far_out, far_in, far_send, far_recv.at[0], peer(0, across))
        far_copy.start()

    with jax.named_scope("backward"):
        loop(0, blocks, backward, True)
        attr_store = pltpu.make_async_copy(attr_grad, attr_out, store_sem.at[0])
        attr_store.start()

    with jax.named_scope("source_sums"):
        high, low = split_bf16(
            jnp.dot(hot_src_t[...], dpre[...], preferred_element_type=jnp.float32)
        )
        sums = lax.dot_general(
            high, wnode[...], NT, preferred_element_type=jnp.float32
        ) + lax.dot_general(low, wnode[...], NT, preferred_element_type=jnp.float32)
        node_own = sums[:rows]
        s_out[...] = sums[rows:].astype(jnp.bfloat16).reshape(n_src - 1, rows, feat)
        far_first(
            n_src,
            lambda k: remote(
                s_out.at[k - 1], s_in.at[k - 1], s_send, s_recv.at[0], y_peer(k)
            ).start(),
        )

    with jax.named_scope("drain"):
        all_of(group.at[pl.ds(0, n_src - 1)], feat_send, feat_recv).wait_send()
        all_of(cot.at[pl.ds(0, n_z - 1), 0], cot_send, cot_recv).wait_send()
        all_of(cot.at[pl.ds(0, 2 * n_z), 0], cz_send, cz_recv).wait_send()
        all_of(cot.at[pl.ds(0, n_z), 0], relay_send, relay_recv).wait_send()
        all_of(cot.at[:, 0], cc_send, cc_recv).wait_send()
        all_of(half_out, half_send, half_recv).wait_send()
        if n_x > 2:
            all_of(x_out, x_send, x_recv).wait_send()
        all_of(b_out, b_send, b_recv).wait_send()
        attr_store.wait()

    with jax.named_scope("last_z"):
        all_of(z_in, z_send, z_recv).wait_recv()
        partial = own[0:rows, :] + jnp.sum(z_in[...].astype(jnp.float32), axis=0)

    with jax.named_scope("last_far"):
        far_copy.wait_recv()
        agg[...] = (partial + far_in[...].astype(jnp.float32)).astype(jnp.bfloat16)
        agg_store = pltpu.make_async_copy(agg, agg_out, store_sem.at[1])
        agg_store.start()

    with jax.named_scope("last_y"):
        all_of(s_in, s_send, s_recv).wait_recv()
        node[...] = (node_own + jnp.sum(s_in[...].astype(jnp.float32), axis=0)).astype(jnp.bfloat16)
        node_store = pltpu.make_async_copy(node, node_out, store_sem.at[2])
        node_store.start()

    with jax.named_scope("drain_last"):
        all_of(z_out, z_send, z_recv).wait_send()
        far_copy.wait_send()
        all_of(s_out, s_send, s_recv).wait_send()
        agg_store.wait()
        node_store.wait()


def write(*refs):
    count = len(refs) // 2
    sem = refs[-1]
    copies = [
        pltpu.make_async_copy(refs[i], refs[count + i], sem.at[i]) for i in range(count)
    ]
    for copy in copies:
        copy.start()
    for copy in copies:
        copy.wait()


def local(
    n_src, n_x, n_z,
    node_feats, cotangent, edge_attr, src_ids, dst_rel, offsets, counts, w_node, w_edge, bias, w_out,
):
    rows, feat = node_feats.shape
    edges, attr_width = edge_attr.shape
    blocks = offsets.shape[0]
    width = edges // blocks
    hidden = w_node.shape[1]
    slab = rows * n_z
    half = slab * n_x
    f32, bf16 = jnp.float32, jnp.bfloat16
    vmem, dma = pltpu.VMEM, pltpu.SemaphoreType.DMA
    anywhere = pl.BlockSpec(memory_space=pl.ANY)
    operands = (
        node_feats, cotangent, edge_attr,
        src_ids.reshape(blocks, width), dst_rel.reshape(blocks, width), offsets, counts,
        w_node, w_edge, bias.reshape(1, hidden), w_out,
    )
    outs = (
        jax.ShapeDtypeStruct((rows, feat), bf16),
        jax.ShapeDtypeStruct((rows, feat), bf16),
        jax.ShapeDtypeStruct((edges, attr_width), bf16),
    )
    results = pl.pallas_call(
        functools.partial(kernel, (n_src, n_x, n_z, rows)),
        out_shape=outs,
        in_specs=[anywhere] * len(operands),
        out_specs=(anywhere,) * 3,
        scratch_shapes=[
            pltpu.SMEM((blocks,), jnp.int32),
            pltpu.SMEM((blocks,), jnp.int32),
            vmem((n_src, rows, feat), bf16),
            vmem((n_z * n_x, CORES, rows, feat), bf16),
            vmem((edges, attr_width), bf16),
            vmem((blocks, width), jnp.int32),
            vmem((blocks, width), jnp.int32),
            vmem(w_node.shape, bf16),
            vmem(w_edge.shape, bf16),
            vmem((1, hidden), f32),
            vmem(w_out.shape, bf16),
            vmem((edges, 2 * width), bf16),
            vmem((n_src * rows, edges), bf16),
            vmem((CORES * half, edges), bf16),
            vmem((edges, WINDOW), bf16),
            vmem((2 * width, hidden), bf16),
            vmem((edges, hidden), f32),
            vmem((edges, feat), bf16),
            vmem((edges, hidden), bf16),
            vmem((edges, attr_width), bf16),
            vmem((half, feat), bf16),
            vmem((half, feat), bf16),
            vmem((half, feat), f32),
            vmem((slab, feat), f32),
            vmem((rows, feat), f32),
            vmem((max(n_x - 2, 1), slab, feat), bf16),
            vmem((max(n_x - 2, 1), slab, feat), bf16),
            vmem((n_z - 1, rows, feat), bf16),
            vmem((n_z - 1, rows, feat), bf16),
            vmem((rows, feat), bf16),
            vmem((rows, feat), bf16),
            vmem((n_z - 1, rows, feat), bf16),
            vmem((n_z - 1, rows, feat), bf16),
            vmem((n_src - 1, rows, feat), bf16),
            vmem((n_src - 1, rows, feat), bf16),
            vmem((rows, feat), bf16),
            vmem((rows, feat), bf16),
            dma((len(operands),)),
            dma((n_x,)),
            dma((3,)),
        ]
        + [dma((1,))] * 21,
        compiler_params=pltpu.CompilerParams(
            collective_id=0, has_side_effects=True, vmem_limit_bytes=32 * 1024 * 1024
        ),
    )(*(pltpu.with_memory_space_constraint(operand, pltpu.HBM) for operand in operands))
    return pl.pallas_call(
        write,
        out_shape=outs,
        in_specs=[anywhere] * 3,
        out_specs=(anywhere,) * 3,
        scratch_shapes=[dma((3,))],
    )(*(pltpu.with_memory_space_constraint(result, pltpu.VMEM) for result in results))


def build(mesh, n_x):
    n_src, n_dst = mesh.shape["src"], mesh.shape["dst"]
    in_specs = (
        P(("dst", "src"), None),
        P(("src", "dst"), None),
        P(("src", "dst"), None),
        P(("src", "dst")),
        P(("src", "dst")),
        P(("src", "dst")),
        P(("src", "dst")),
        P(),
        P(),
        P(),
        P(),
    )
    out_specs = (P(("src", "dst"), None), P(("dst", "src"), None), P(("src", "dst"), None))
    return jax.shard_map(
        functools.partial(local, n_src, n_x, n_dst // (n_x * CORES)),
        mesh=mesh, in_specs=in_specs, out_specs=out_specs, check_vma=False,
    )


def solution(mesh):
    return build(mesh, X_CHIPS)
```

time: 421 us -> 45.4 us (0.11)
  the two profiles are of different devices: /device:TPU:16 before, /device:TPU:1 now
where the time goes in v2:
time: 45.4 us; the launch traced here: 45.3 us
  Pallas kernels  44.6 us (98%)
  between operations  0.64 us (1%)
    pallas_call x1, Pallas kernels, local(): pl.pallas_call(functools.partial(kernel, (n_src, n_x, n_z, rows)), out_sh...  43.8 us

profile of v2, /device:TPU:1, one launch (start us, length us, event | category | flops | bytes accessed | tf_op | source)
XLA Modules:
  0.0 45.3 jit_solution(8425489884164002323)
XLA Ops:
  0.6 43.8 %shard_map.130 = (bf16[16,256]{1,0:T(8,128)(2,1)S(1)}, bf16[16,256]{1,0:T(8,128)(2,1)S(1)}, bf16[1536,128]{1,0:T(8,128)(2,1)S(1)}) custom-call(bf16[16,256]{1,0:T(8,128)(2,1)} %feats_in.1, bf16[16,256]{1,0:T(8,128)(2,1)} %cot_in.1, bf16[1536,128]{1,0:T(8,128)(2,1)} %attr_in.1, s32[12,128]{1,0:T(8,128)} %bitcast.3, s32[12,128]{1,0:T(8,128)} %bitcast.4, ...), custom_call_target="tpu_custom_call" | custom-call | tf_op jit(solution)/shard_map/pallas_call | solution.py:403
  44.5 0.8 %shard_map.131 = (bf16[16,256]{1,0:T(8,128)(2,1)}, bf16[16,256]{1,0:T(8,128)(2,1)}, bf16[1536,128]{1,0:T(8,128)(2,1)}) custom-call(bf16[16,256]{1,0:T(8,128)(2,1)S(1)} %get-tuple-element.6.refs_0_, bf16[16,256]{1,0:T(8,128)(2,1)S(1)} %get-tuple-element.7.refs_1_, bf16[1536,128]{1,0:T(8,128)(2,1)S(1)} %get-tuple-element.8.refs_2_), custom_call_target="tpu_custom_call" | custom-call | tf_op jit(solution)/shard_map/pallas_call | solution.py:455

commit v3 on v2

--- a/solution.py
+++ b/solution.py
@@ -42,11 +42,11 @@
     agg_out, node_out, attr_out,
     offsets, counts, group, cot, attr, src, rel, wnode, wedge, bias, wout,
     hot_src, hot_src_t, hot_dst, hot_win,
-    proj, pre, msg, dpre, attr_grad,
+    proj, pre, msg, hidden, attr_grad,
     half_out, half_in, kept, own, far, x_out, x_in, b_out, b_in, far_out, far_in, z_out, z_in, s_out, s_in,
     agg, node,
-    load_sem, half_recv, store_sem,
-    feat_send, feat_recv, cot_send, cot_recv, cz_send, cz_recv, relay_send, relay_recv, cc_send, cc_recv, half_send,
+    load_sem, half_recv, store_sem, cot_recv, cz_recv,
+    feat_send, feat_recv, cot_send, cz_send, relay_send, relay_recv, cc_send, cc_recv, half_send,
     x_send, x_recv, b_send, b_recv, far_send, far_recv, z_send, z_recv, s_send, s_recv,
 ):
     n_src, n_x, n_z, rows = dims
@@ -61,6 +61,8 @@
     slab = rows * n_z
     half = slab * n_x
     across = n_x // 2
+    reach = n_z // 4
+    near = 2 * reach + 1
 
     def dst_at(z, x, c):
         return (z * n_x + x) * CORES + c
@@ -121,13 +123,39 @@
             n_src, lambda k: remote(mine, mine, feat_send, feat_recv.at[0], y_peer(k)).start()
         )
 
-        def cot_at(z, x):
+        def cot_at(j, x):
+            z = lax.rem(me_z + (n_z - reach) + j, n_z)
             return cot.at[z * n_x + lax.rem(me_x + x + n_x, n_x), me_c]
 
-        def send_cot(z, x, send, recv, device):
-            remote(cot_at(z, x), cot_at(z, x), send, recv.at[0], device).start()
-
-        far_first(n_z, lambda k: send_cot(me_z, 0, cot_send, cot_recv, peer(k, 0)))
+        def send_cot(j, x, send, recv, device):
+            remote(cot_at(j, x), cot_at(j, x), send, recv, device).start()
+
+        def cot_bytes(count, send, recv):
+            return remote(cot.at[pl.ds(0, count), 0], cot.at[pl.ds(0, count), 0], send, recv, sibling)
+
+        def to_sibling(j, x):
+            send_cot(j, x, cc_send, cc_recv.at[0], sibling)
+
+        for k in range(reach, 0, -1):
+            send_cot(reach, 0, cot_send, cot_recv.at[0], peer(k, 0))
+            send_cot(reach, 0, cot_send, cot_recv.at[0], peer(-k, 0))
+        loop(
+            reach + 1,
+            n_z - reach,
+            lambda k: send_cot(reach, 0, cot_send, cot_recv.at[1], peer(k, 0)),
+        )
+
+        def second(j):
+            send_cot(j, 0, cz_send, cz_recv.at[0], peer(0, 1))
+            send_cot(j, 0, cz_send, cz_recv.at[0], peer(0, -1))
+
+        def second_far(j):
+            for k in (across, 1, -1):
+                send_cot(j, 0, cz_send, cz_recv.at[1], peer(0, k))
+
+        def pass_beside(j):
+            to_sibling(j, -1)
+            to_sibling(j, 1)
 
     with jax.named_scope("marks"):
         for i in (2, 3, 4, 5):
@@ -160,8 +188,8 @@
             hot_dst[:, here] = hot(tall == jnp.where(valid, place, -1))
             base = jnp.minimum(start >> 5, last_window) * (CORES * rows)
             inside = jnp.broadcast_to(jnp.where(valid, target - base, -1), (width, width)).T
-            hot_win[here, 0:width] = hot(inside == lane)
-            hot_win[here, width : 2 * width] = hot(inside == lane + width)
+            hot_win[here, 0:width] = 0.5 * hot(inside == lane)
+            hot_win[here, width : 2 * width] = 0.5 * hot(inside == lane + width)
 
         loop(0, blocks, mark)
 
@@ -172,7 +200,7 @@
 
         def attr_part(i):
             here = pl.ds(pl.multiple_of(i * tile, tile), tile)
-            pre[here, :] = (
+            pre[here, :] = 0.5 * (
                 jnp.dot(attr[here, :], wedge[...], preferred_element_type=jnp.float32) + bias[...]
             )
 
@@ -185,7 +213,8 @@
 
     with jax.named_scope("forward"):
         high, low = split_bf16(
-            jnp.dot(
+            0.5
+            * jnp.dot(
                 group[...].reshape(n_src * rows, feat), wnode[...], preferred_element_type=jnp.float32
             )
         )
@@ -194,19 +223,38 @@
         proj[0 : n_src * rows, :] = high
         proj[width : width + n_src * rows, :] = low
 
-        def forward(i):
-            here = pl.ds(pl.multiple_of(i * tile, tile), tile)
+        def activate(i):
+            here = slice(i * tile, (i + 1) * tile)
             value = pre[here, :] + jnp.dot(
                 hot_src[here, :], proj[...], preferred_element_type=jnp.float32
             )
-            sig = 0.5 * jnp.tanh(0.5 * value) + 0.5
-            hidden = (value * sig).astype(jnp.bfloat16)
-            pre[here, :] = sig * (1.0 + value * (1.0 - sig))
-            msg[here, :] = jnp.dot(hidden, wout[...], preferred_element_type=jnp.float32).astype(
-                jnp.bfloat16
-            )
-
-        loop(0, edges // tile, forward, True)
+            rise = 1.0 + jnp.tanh(value)
+            silu = value * rise
+            hidden[here, :] = silu.astype(jnp.bfloat16)
+            pre[here, :] = rise + silu * (2.0 - rise)
+
+        def project(i):
+            here = slice(i * tile, (i + 1) * tile)
+            msg[here, :] = jnp.dot(
+                hidden[here, :], wout[...], preferred_element_type=jnp.float32
+            ).astype(jnp.bfloat16)
+
+        tiles = edges // tile
+        early = tiles // 3
+        for i in range(early):
+            activate(i)
+
+    with jax.named_scope("cot_near"):
+        cot_bytes(near - 1, cot_send, cot_recv.at[0]).wait_recv()
+        loop(0, near, second)
+        loop(0, near, lambda j: to_sibling(j, 0))
+
+    with jax.named_scope("forward_rest"):
+        for i in range(early, tiles):
+            activate(i)
+            project(i - early)
+        for i in range(tiles - early, tiles):
+            project(i)
 
     with jax.named_scope("sums"):
         order = (across,) + tuple(k for k in range(1, n_x) if k != across) + (0,)
@@ -215,24 +263,36 @@
             part = pl.ds(k * slab, slab)
             return remote(half_out.at[part], half_in.at[part], half_send, half_recv.at[k], sibling)
 
-        half_out[...] = jnp.dot(
-            hot_dst[half : 2 * half, :], msg[...], preferred_element_type=jnp.float32
-        ).astype(jnp.bfloat16)
+        piece = half // 2
+
+        def gather_half(i):
+            here = pl.ds(pl.multiple_of(i * piece, piece), piece)
+            there = pl.ds(pl.multiple_of(half + i * piece, piece), piece)
+            half_out[here, :] = jnp.dot(
+                hot_dst[there, :], msg[...], preferred_element_type=jnp.float32
+            ).astype(jnp.bfloat16)
+
+        loop(0, 2, gather_half)
         for k in order:
             half_copy(k).start()
 
-    with jax.named_scope("cot_second"):
-        all_of(cot.at[pl.ds(0, n_z - 1), 0], cot_send, cot_recv).wait_recv()
-
-        def second(z):
-            send_cot(z, 0, cz_send, cz_recv, peer(0, 1))
-            send_cot(z, 0, cz_send, cz_recv, peer(0, -1))
-
-        loop(0, n_z, second)
-        loop(0, n_z, lambda z: send_cot(z, 0, cc_send, cc_recv, sibling))
+    with jax.named_scope("cot_far"):
+        cot_bytes(n_z - near, cot_send, cot_recv.at[1]).wait_recv()
+        loop(near, n_z, second_far)
 
     with jax.named_scope("sums_rest"):
-        kept[...] = jnp.dot(hot_dst[0:half, :], msg[...], preferred_element_type=jnp.float32)
+        def gather_kept(i):
+            here = pl.ds(pl.multiple_of(i * piece, piece), piece)
+            kept[here, :] = jnp.dot(hot_dst[here, :], msg[...], preferred_element_type=jnp.float32)
+
+        loop(0, 2, gather_kept)
+
+    with jax.named_scope("cot_third"):
+        cot_bytes(2 * near, cz_send, cz_recv.at[0]).wait_recv()
+        loop(0, near // 2, lambda j: send_cot(j, -1, relay_send, relay_recv.at[0], peer(0, 1)))
+        loop(near // 2, near, lambda j: send_cot(j, 1, relay_send, relay_recv.at[0], peer(0, -1)))
+
+    with jax.named_scope("sums_both"):
         slot = 0
         for k in order:
             part = slice(k * slab, (k + 1) * slab)
@@ -254,30 +314,20 @@
             else:
                 own[...] = total
 
-    with jax.named_scope("cot_third"):
-        all_of(cot.at[pl.ds(0, 2 * n_z), 0], cz_send, cz_recv).wait_recv()
-        loop(0, n_z // 2, lambda z: send_cot(z, -1, relay_send, relay_recv, peer(0, 1)))
-        loop(n_z // 2, n_z, lambda z: send_cot(z, 1, relay_send, relay_recv, peer(0, -1)))
-
-        def pass_beside(z):
-            send_cot(z, -1, cc_send, cc_recv, sibling)
-            send_cot(z, 1, cc_send, cc_recv, sibling)
-
-        loop(0, n_z, pass_beside)
-
-    def backward(b):
-        here = pl.ds(pl.multiple_of(b * width, width), width)
-        first = jnp.minimum(offsets[b] >> 5, last_window)
-        window = cot[pl.ds(first, WINDOW // (CORES * rows))].reshape(WINDOW, feat)
-        d_message = jnp.dot(
-            hot_win[here, :], window, preferred_element_type=jnp.float32
-        ).astype(jnp.bfloat16)
-        d_hidden = lax.dot_general(d_message, wout[...], NT, preferred_element_type=jnp.float32)
-        d_pre = (d_hidden * pre[here, :]).astype(jnp.bfloat16)
-        dpre[here, :] = d_pre
-        attr_grad[here, :] = lax.dot_general(
-            d_pre, wedge[...], NT, preferred_element_type=jnp.float32
-        ).astype(jnp.bfloat16)
+    with jax.named_scope("cot_rest"):
+        loop(near, n_z, lambda j: to_sibling(j, 0))
+        loop(0, near, pass_beside)
+        cot_bytes(near, relay_send, relay_recv.at[0]).wait_recv()
+        loop(0, near, lambda j: to_sibling(j, across))
+
+    with jax.named_scope("cot_rest_far"):
+        cot_bytes((n_x - 1) * (n_z - near), cz_send, cz_recv.at[1]).wait_recv()
+
+        def pass_far(j):
+            for k in (across, 1, -1):
+                to_sibling(j, k)
+
+        loop(near, n_z, pass_far)
 
     with jax.named_scope("sums_x"):
         if n_x > 2:
@@ -294,27 +344,30 @@
             ).start(),
         )
 
-    with jax.named_scope("cot_rest"):
-        all_of(cot.at[pl.ds(0, n_z), 0], relay_send, relay_recv).wait_recv()
-        loop(0, n_z, lambda z: send_cot(z, across, cc_send, cc_recv, sibling))
-
     with jax.named_scope("cot_last"):
         all_of(cot.at[:, 0], cc_send, cc_recv).wait_recv()
 
-    with jax.named_scope("sums_far"):
-        all_of(b_in, b_send, b_recv).wait_recv()
-        far_out[...] = (far[...] + jnp.sum(b_in[...].astype(jnp.float32), axis=0)).astype(jnp.bfloat16)
-        far_copy = remote(far_out, far_in, far_send, far_recv.at[0], peer(0, across))
-        far_copy.start()
-
     with jax.named_scope("backward"):
-        loop(0, blocks, backward, True)
-        attr_store = pltpu.make_async_copy(attr_grad, attr_out, store_sem.at[0])
-        attr_store.start()
+        for i in range(blocks):
+            here = slice(i * width, (i + 1) * width)
+            first = jnp.minimum(offsets[i] >> 5, last_window)
+            window = cot[pl.ds(first, WINDOW // (CORES * rows))].reshape(WINDOW, feat)
+            msg[here, :] = jnp.dot(
+                hot_win[here, :], window, preferred_element_type=jnp.float32
+            ).astype(jnp.bfloat16)
+
+    with jax.named_scope("d_pre"):
+        wide = min(512, edges)
+        for i in range(edges // wide):
+            here = slice(i * wide, (i + 1) * wide)
+            d_hidden = lax.dot_general(
+                msg[here, :], wout[...], NT, preferred_element_type=jnp.float32
+            )
+            hidden[here, :] = (d_hidden * pre[here, :]).astype(jnp.bfloat16)
 
     with jax.named_scope("source_sums"):
         high, low = split_bf16(
-            jnp.dot(hot_src_t[...], dpre[...], preferred_element_type=jnp.float32)
+            jnp.dot(hot_src_t[...], hidden[...], preferred_element_type=jnp.float32)
         )
         sums = lax.dot_general(
             high, wnode[...], NT, preferred_element_type=jnp.float32
@@ -328,17 +381,31 @@
             ).start(),
         )
 
+    with jax.named_scope("sums_far"):
+        all_of(b_in, b_send, b_recv).wait_recv()
+        far_out[...] = (far[...] + jnp.sum(b_in[...].astype(jnp.float32), axis=0)).astype(jnp.bfloat16)
+        far_copy = remote(far_out, far_in, far_send, far_recv.at[0], peer(0, across))
+        far_copy.start()
+
+    with jax.named_scope("attr_grads"):
+        for i in range(edges // wide):
+            here = slice(i * wide, (i + 1) * wide)
+            attr_grad[here, :] = lax.dot_general(
+                hidden[here, :], wedge[...], NT, preferred_element_type=jnp.float32
+            ).astype(jnp.bfloat16)
+        attr_store = pltpu.make_async_copy(attr_grad, attr_out, store_sem.at[0])
+        attr_store.start()
+
     with jax.named_scope("drain"):
         all_of(group.at[pl.ds(0, n_src - 1)], feat_send, feat_recv).wait_send()
-        all_of(cot.at[pl.ds(0, n_z - 1), 0], cot_send, cot_recv).wait_send()
-        all_of(cot.at[pl.ds(0, 2 * n_z), 0], cz_send, cz_recv).wait_send()
-        all_of(cot.at[pl.ds(0, n_z), 0], relay_send, relay_recv).wait_send()
+        cot_bytes(n_z - 1, cot_send, cot_recv.at[0]).wait_send()
+        cot_bytes(2 * near + (n_x - 1) * (n_z - near), cz_send, cz_recv.at[0]).wait_send()
+        cot_bytes(near, relay_send, relay_recv.at[0]).wait_send()
         all_of(cot.at[:, 0], cc_send, cc_recv).wait_send()
         all_of(half_out, half_send, half_recv).wait_send()
         if n_x > 2:
             all_of(x_out, x_send, x_recv).wait_send()
         all_of(b_out, b_send, b_recv).wait_send()
-        attr_store.wait()
 
     with jax.named_scope("last_z"):
         all_of(z_in, z_send, z_recv).wait_recv()
@@ -360,6 +427,7 @@
         all_of(z_out, z_send, z_recv).wait_send()
         far_copy.wait_send()
         all_of(s_out, s_send, s_recv).wait_send()
+        attr_store.wait()
         agg_store.wait()
         node_store.wait()
 
@@ -446,8 +514,10 @@
             dma((len(operands),)),
             dma((n_x,)),
             dma((3,)),
+            dma((2,)),
+            dma((2,)),
         ]
-        + [dma((1,))] * 21,
+        + [dma((1,))] * 19,
         compiler_params=pltpu.CompilerParams(
             collective_id=0, has_side_effects=True, vmem_limit_bytes=32 * 1024 * 1024
         ),

time: 45.4 us -> 42 us (0.925)
  Pallas kernels: 44.6 us -> 41.2 us
    pallas_call x1, Pallas kernels: 43.8 us -> 40.5 us  [local(): pl.pallas_call(functools.partial(kernel, (n_src, n_x, n_z, rows)), out_sh...]
where the time goes in v3:
time: 42 us; the launch traced here: 41.9 us
  Pallas kernels  41.2 us (98%)
  between operations  0.64 us (2%)
    pallas_call x1, Pallas kernels, local(): pl.pallas_call(functools.partial(kernel, (n_src, n_x, n_z, rows)), out_sh...  40.5 us

profile of v3, /device:TPU:1, one launch (start us, length us, event | category | flops | bytes accessed | tf_op | source)
XLA Modules:
  0.0 41.9 jit_solution(7151676507529696049)
XLA Ops:
  0.6 40.5 %shard_map.130 = (bf16[16,256]{1,0:T(8,128)(2,1)S(1)}, bf16[16,256]{1,0:T(8,128)(2,1)S(1)}, bf16[1536,128]{1,0:T(8,128)(2,1)S(1)}) custom-call(bf16[16,256]{1,0:T(8,128)(2,1)} %feats_in.1, bf16[16,256]{1,0:T(8,128)(2,1)} %cot_in.1, bf16[1536,128]{1,0:T(8,128)(2,1)} %attr_in.1, s32[12,128]{1,0:T(8,128)} %bitcast.3, s32[12,128]{1,0:T(8,128)} %bitcast.4, ...), custom_call_target="tpu_custom_call" | custom-call | tf_op jit(solution)/shard_map/pallas_call | solution.py:471
  41.1 0.8 %shard_map.131 = (bf16[16,256]{1,0:T(8,128)(2,1)}, bf16[16,256]{1,0:T(8,128)(2,1)}, bf16[1536,128]{1,0:T(8,128)(2,1)}) custom-call(bf16[16,256]{1,0:T(8,128)(2,1)S(1)} %get-tuple-element.6.refs_0_, bf16[16,256]{1,0:T(8,128)(2,1)S(1)} %get-tuple-element.7.refs_1_, bf16[1536,128]{1,0:T(8,128)(2,1)S(1)} %get-tuple-element.8.refs_2_), custom_call_target="tpu_custom_call" | custom-call | tf_op jit(solution)/shard_map/pallas_call | solution.py:525

commit v4 on v3

--- a/solution.py
+++ b/solution.py
@@ -68,7 +68,7 @@
         return (z * n_x + x) * CORES + c
 
     def y_peer(k):
-        return (lax.rem(me_s + k, n_src), me_d)
+        return (lax.rem(me_s + k + n_src, n_src), me_d)
 
     def peer(z, x):
         return (
@@ -92,8 +92,8 @@
             pltpu.make_async_copy(source, target, load_sem.at[i])
             for i, (source, target) in enumerate(
                 (
+                    (src_in, src), (rel_in, rel), (offsets_in, offsets), (counts_in, counts),
                     (feats_in, group.at[me_s]), (cot_in, cot.at[me_z * n_x + me_x, me_c]),
-                    (src_in, src), (rel_in, rel), (offsets_in, offsets), (counts_in, counts),
                     (attr_in, attr), (wedge_in, wedge), (bias_in, bias),
                     (wnode_in, wnode), (wout_in, wout),
                 )
@@ -102,63 +102,22 @@
         for load in loads:
             load.start()
 
-    with jax.named_scope("barrier"):
+    with jax.named_scope("greet"):
         barrier = pltpu.get_barrier_semaphore()
 
         def greet(device):
             pl.semaphore_signal(barrier, inc=1, device_id=device, device_id_type=MESH)
 
         far_first(n_src, lambda k: greet(y_peer(k)))
-        far_first(n_z, lambda k: greet(peer(k, 0)))
+        for k in range(reach, 0, -1):
+            greet(peer(k, 0))
+            greet(peer(-k, 0))
         for k in range(1, n_x):
             greet(peer(0, k))
         greet(sibling)
-        loads[0].wait()
-        loads[1].wait()
-        pl.semaphore_wait(barrier, (n_src - 1) + (n_z - 1) + (n_x - 1) + 1)
-
-    with jax.named_scope("first_sends"):
-        mine = group.at[me_s]
-        far_first(
-            n_src, lambda k: remote(mine, mine, feat_send, feat_recv.at[0], y_peer(k)).start()
-        )
-
-        def cot_at(j, x):
-            z = lax.rem(me_z + (n_z - reach) + j, n_z)
-            return cot.at[z * n_x + lax.rem(me_x + x + n_x, n_x), me_c]
-
-        def send_cot(j, x, send, recv, device):
-            remote(cot_at(j, x), cot_at(j, x), send, recv, device).start()
-
-        def cot_bytes(count, send, recv):
-            return remote(cot.at[pl.ds(0, count), 0], cot.at[pl.ds(0, count), 0], send, recv, sibling)
-
-        def to_sibling(j, x):
-            send_cot(j, x, cc_send, cc_recv.at[0], sibling)
-
-        for k in range(reach, 0, -1):
-            send_cot(reach, 0, cot_send, cot_recv.at[0], peer(k, 0))
-            send_cot(reach, 0, cot_send, cot_recv.at[0], peer(-k, 0))
-        loop(
-            reach + 1,
-            n_z - reach,
-            lambda k: send_cot(reach, 0, cot_send, cot_recv.at[1], peer(k, 0)),
-        )
-
-        def second(j):
-            send_cot(j, 0, cz_send, cz_recv.at[0], peer(0, 1))
-            send_cot(j, 0, cz_send, cz_recv.at[0], peer(0, -1))
-
-        def second_far(j):
-            for k in (across, 1, -1):
-                send_cot(j, 0, cz_send, cz_recv.at[1], peer(0, k))
-
-        def pass_beside(j):
-            to_sibling(j, -1)
-            to_sibling(j, 1)
-
-    with jax.named_scope("marks"):
-        for i in (2, 3, 4, 5):
+
+    with jax.named_scope("marks_first"):
+        for i in range(4):
             loads[i].wait()
         lane = lax.broadcasted_iota(jnp.int32, (width, width), 1)
         sub = lax.broadcasted_iota(jnp.int32, (width, width), 0)
@@ -191,7 +150,49 @@
             hot_win[here, 0:width] = 0.5 * hot(inside == lane)
             hot_win[here, width : 2 * width] = 0.5 * hot(inside == lane + width)
 
-        loop(0, blocks, mark)
+        loop(0, blocks // 4, mark)
+
+    with jax.named_scope("barrier"):
+        loads[4].wait()
+        loads[5].wait()
+        pl.semaphore_wait(barrier, (n_src - 1) + 2 * reach + (n_x - 1) + 1)
+
+    with jax.named_scope("first_sends"):
+        def cot_at(j, x):
+            z = lax.rem(me_z + (n_z - reach) + j, n_z)
+            return cot.at[z * n_x + lax.rem(me_x + x + n_x, n_x), me_c]
+
+        def send_cot(j, x, send, recv, device):
+            remote(cot_at(j, x), cot_at(j, x), send, recv, device).start()
+
+        def cot_bytes(count, send, recv):
+            return remote(cot.at[pl.ds(0, count), 0], cot.at[pl.ds(0, count), 0], send, recv, sibling)
+
+        def to_sibling(j, x):
+            send_cot(j, x, cc_send, cc_recv.at[0], sibling)
+
+        for k in range(reach, 0, -1):
+            send_cot(reach, 0, cot_send, cot_recv.at[0], peer(k, 0))
+            send_cot(reach, 0, cot_send, cot_recv.at[0], peer(-k, 0))
+        mine = group.at[me_s]
+        far_first(
+            n_src, lambda k: remote(mine, mine, feat_send, feat_recv.at[0], y_peer(k)).start()
+        )
+
+        def second(j):
+            send_cot(j, 0, cz_send, cz_recv.at[0], peer(0, 1))
+            send_cot(j, 0, cz_send, cz_recv.at[0], peer(0, -1))
+
+        def second_far(j):
+            for k in (across, 1, -1):
+                send_cot(j, 0, cz_send, cz_recv.at[1], peer(0, k))
+
+        def pass_beside(j):
+            to_sibling(j, -1)
+            to_sibling(j, 1)
+
+    with jax.named_scope("marks"):
+        loop(blocks // 4, blocks, mark)
 
     with jax.named_scope("attr_part"):
         for i in (6, 7, 8):
@@ -205,6 +206,15 @@
             )
 
         loop(0, edges // tile, attr_part, True)
+
+    with jax.named_scope("cot_near"):
+        cot_bytes(near - 1, cot_send, cot_recv.at[0]).wait_recv()
+        for o in range(reach, 0, -1):
+            send_cot(reach + o, 0, cot_send, cot_recv.at[1], peer(-reach, 0))
+        for o in range(n_z - 3 * reach - 1, 0, -1):
+            send_cot(reach - o, 0, cot_send, cot_recv.at[1], peer(reach, 0))
+        loop(0, near, second)
+        loop(0, near, lambda j: to_sibling(j, 0))
 
     with jax.named_scope("feats_wait"):
         loads[9].wait()
@@ -240,45 +250,29 @@
             ).astype(jnp.bfloat16)
 
         tiles = edges // tile
-        early = tiles // 3
-        for i in range(early):
+        activate(0)
+        for i in range(1, tiles):
             activate(i)
-
-    with jax.named_scope("cot_near"):
-        cot_bytes(near - 1, cot_send, cot_recv.at[0]).wait_recv()
-        loop(0, near, second)
-        loop(0, near, lambda j: to_sibling(j, 0))
-
-    with jax.named_scope("forward_rest"):
-        for i in range(early, tiles):
-            activate(i)
-            project(i - early)
-        for i in range(tiles - early, tiles):
-            project(i)
+            project(i - 1)
+        project(tiles - 1)
 
     with jax.named_scope("sums"):
-        order = (across,) + tuple(k for k in range(1, n_x) if k != across) + (0,)
-
-        def half_copy(k):
-            part = pl.ds(k * slab, slab)
-            return remote(half_out.at[part], half_in.at[part], half_send, half_recv.at[k], sibling)
-
         piece = half // 2
 
+        def half_copy(j):
+            part = pl.ds(pl.multiple_of(j * piece, piece), piece)
+            return remote(half_out.at[part], half_in.at[part], half_send, half_recv.at[j], sibling)
+
         def gather_half(i):
-            here = pl.ds(pl.multiple_of(i * piece, piece), piece)
-            there = pl.ds(pl.multiple_of(half + i * piece, piece), piece)
+            j = 1 - i
+            here = pl.ds(pl.multiple_of(j * piece, piece), piece)
+            there = pl.ds(pl.multiple_of(half + j * piece, piece), piece)
             half_out[here, :] = jnp.dot(
                 hot_dst[there, :], msg[...], preferred_element_type=jnp.float32
             ).astype(jnp.bfloat16)
+            half_copy(j).start()
 
         loop(0, 2, gather_half)
-        for k in order:
-            half_copy(k).start()
-
-    with jax.named_scope("cot_far"):
-        cot_bytes(n_z - near, cot_send, cot_recv.at[1]).wait_recv()
-        loop(near, n_z, second_far)
 
     with jax.named_scope("sums_rest"):
         def gather_kept(i):
@@ -289,14 +283,21 @@
 
     with jax.named_scope("cot_third"):
         cot_bytes(2 * near, cz_send, cz_recv.at[0]).wait_recv()
-        loop(0, near // 2, lambda j: send_cot(j, -1, relay_send, relay_recv.at[0], peer(0, 1)))
-        loop(near // 2, near, lambda j: send_cot(j, 1, relay_send, relay_recv.at[0], peer(0, -1)))
+        loop(0, near, lambda j: send_cot(j, 1, relay_send, relay_recv.at[0], peer(0, -1)))
+
+    with jax.named_scope("cot_far"):
+        cot_bytes(n_z - near, cot_send, cot_recv.at[1]).wait_recv()
+        loop(near, n_z, second_far)
 
     with jax.named_scope("sums_both"):
+        order = tuple(range(across, n_x)) + tuple(range(across - 1, -1, -1))
         slot = 0
         for k in order:
             part = slice(k * slab, (k + 1) * slab)
-            half_copy(k).wait_recv()
+            if k == across:
+                half_copy(1).wait_recv()
+            if k == across - 1:
+                half_copy(0).wait_recv()
             total = kept[part, :] + half_in[part, :].astype(jnp.float32)
             if k == across:
                 far[...] = total[:rows]

time: 42 us -> 40.3 us (0.960)
  Pallas kernels: 41.2 us -> 39.5 us
    pallas_call x1, Pallas kernels: 40.5 us -> 38.7 us  [local(): pl.pallas_call(functools.partial(kernel, (n_src, n_x, n_z, rows)), out_sh...]
where the time goes in v4:
time: 40.3 us; the launch traced here: 40.1 us
  Pallas kernels  39.5 us (98%)
  between operations  0.64 us (2%)
    pallas_call x1, Pallas kernels, local(): pl.pallas_call(functools.partial(kernel, (n_src, n_x, n_z, rows)), out_sh...  38.7 us

profile of v4, /device:TPU:1, one launch (start us, length us, event | category | flops | bytes accessed | tf_op | source)
XLA Modules:
  0.0 40.1 jit_solution(8634554446965659725)
XLA Ops:
  0.6 38.7 %shard_map.130 = (bf16[16,256]{1,0:T(8,128)(2,1)S(1)}, bf16[16,256]{1,0:T(8,128)(2,1)S(1)}, bf16[1536,128]{1,0:T(8,128)(2,1)S(1)}) custom-call(bf16[16,256]{1,0:T(8,128)(2,1)} %feats_in.1, bf16[16,256]{1,0:T(8,128)(2,1)} %cot_in.1, bf16[1536,128]{1,0:T(8,128)(2,1)} %attr_in.1, s32[12,128]{1,0:T(8,128)} %bitcast.3, s32[12,128]{1,0:T(8,128)} %bitcast.4, ...), custom_call_target="tpu_custom_call" | custom-call | tf_op jit(solution)/shard_map/pallas_call | solution.py:472
  39.3 0.8 %shard_map.131 = (bf16[16,256]{1,0:T(8,128)(2,1)}, bf16[16,256]{1,0:T(8,128)(2,1)}, bf16[1536,128]{1,0:T(8,128)(2,1)}) custom-call(bf16[16,256]{1,0:T(8,128)(2,1)S(1)} %get-tuple-element.6.refs_0_, bf16[16,256]{1,0:T(8,128)(2,1)S(1)} %get-tuple-element.7.refs_1_, bf16[1536,128]{1,0:T(8,128)(2,1)S(1)} %get-tuple-element.8.refs_2_), custom_call_target="tpu_custom_call" | custom-call | tf_op jit(solution)/shard_map/pallas_call | solution.py:526

commit v5 on v4

--- a/solution.py
+++ b/solution.py
@@ -43,7 +43,7 @@
     offsets, counts, group, cot, attr, src, rel, wnode, wedge, bias, wout,
     hot_src, hot_src_t, hot_dst, hot_win,
     proj, pre, msg, hidden, attr_grad,
-    half_out, half_in, kept, own, far, x_out, x_in, b_out, b_in, far_out, far_in, z_out, z_in, s_out, s_in,
+    half_out, half_in, kept, own, x_out, x_in, b_out, b_in, far_out, far_in, z_out, z_in, s_out, s_in,
     agg, node,
     load_sem, half_recv, store_sem, cot_recv, cz_recv,
     feat_send, feat_recv, cot_send, cz_send, relay_send, relay_recv, cc_send, cc_recv, half_send,
@@ -214,7 +214,6 @@
         for o in range(n_z - 3 * reach - 1, 0, -1):
             send_cot(reach - o, 0, cot_send, cot_recv.at[1], peer(reach, 0))
         loop(0, near, second)
-        loop(0, near, lambda j: to_sibling(j, 0))
 
     with jax.named_scope("feats_wait"):
         loads[9].wait()
@@ -274,13 +273,6 @@
 
         loop(0, 2, gather_half)
 
-    with jax.named_scope("sums_rest"):
-        def gather_kept(i):
-            here = pl.ds(pl.multiple_of(i * piece, piece), piece)
-            kept[here, :] = jnp.dot(hot_dst[here, :], msg[...], preferred_element_type=jnp.float32)
-
-        loop(0, 2, gather_kept)
-
     with jax.named_scope("cot_third"):
         cot_bytes(2 * near, cz_send, cz_recv.at[0]).wait_recv()
         loop(0, near, lambda j: send_cot(j, 1, relay_send, relay_recv.at[0], peer(0, -1)))
@@ -289,34 +281,32 @@
         cot_bytes(n_z - near, cot_send, cot_recv.at[1]).wait_recv()
         loop(near, n_z, second_far)
 
+    with jax.named_scope("sums_rest"):
+        def gather_kept(i):
+            j = 1 - i
+            here = pl.ds(pl.multiple_of(j * piece, piece), piece)
+            total = jnp.dot(hot_dst[here, :], msg[...], preferred_element_type=jnp.float32)
+            half_copy(j).wait_recv()
+            total = total + half_in[here, :].astype(jnp.float32)
+            kept[j] = total[:slab]
+            x_out[j] = total[slab:].astype(jnp.bfloat16)
+            remote(
+                x_out.at[j], x_in.at[j], x_send, x_recv.at[0], peer(0, 2 * j + 1)
+            ).start()
+
+        loop(0, 2, gather_kept)
+
     with jax.named_scope("sums_both"):
-        order = tuple(range(across, n_x)) + tuple(range(across - 1, -1, -1))
-        slot = 0
-        for k in order:
-            part = slice(k * slab, (k + 1) * slab)
-            if k == across:
-                half_copy(1).wait_recv()
-            if k == across - 1:
-                half_copy(0).wait_recv()
-            total = kept[part, :] + half_in[part, :].astype(jnp.float32)
-            if k == across:
-                far[...] = total[:rows]
-                b_out[...] = total[rows:].astype(jnp.bfloat16).reshape(n_z - 1, rows, feat)
-                far_first(
-                    n_z,
-                    lambda z: remote(
-                        b_out.at[z - 1], b_in.at[z - 1], b_send, b_recv.at[0], peer(z, 0)
-                    ).start(),
-                )
-            elif k:
-                x_out[slot] = total.astype(jnp.bfloat16)
-                remote(x_out.at[slot], x_in.at[slot], x_send, x_recv.at[0], peer(0, k)).start()
-                slot += 1
-            else:
-                own[...] = total
+        b_out[...] = kept[1, rows:, :].astype(jnp.bfloat16).reshape(n_z - 1, rows, feat)
+        far_first(
+            n_z,
+            lambda z: remote(
+                b_out.at[z - 1], b_in.at[z - 1], b_send, b_recv.at[0], peer(z, 0)
+            ).start(),
+        )
 
     with jax.named_scope("cot_rest"):
-        loop(near, n_z, lambda j: to_sibling(j, 0))
+        loop(0, n_z, lambda j: to_sibling(j, 0))
         loop(0, near, pass_beside)
         cot_bytes(near, relay_send, relay_recv.at[0]).wait_recv()
         loop(0, near, lambda j: to_sibling(j, across))
@@ -333,7 +323,7 @@
     with jax.named_scope("sums_x"):
         if n_x > 2:
             all_of(x_in, x_send, x_recv).wait_recv()
-        summed = own[...]
+        summed = kept[0]
         for k in range(n_x - 2):
             summed = summed + x_in[k].astype(jnp.float32)
         own[...] = summed
@@ -384,7 +374,7 @@
 
     with jax.named_scope("sums_far"):
         all_of(b_in, b_send, b_recv).wait_recv()
-        far_out[...] = (far[...] + jnp.sum(b_in[...].astype(jnp.float32), axis=0)).astype(jnp.bfloat16)
+        far_out[...] = (kept[1, :rows, :] + jnp.sum(b_in[...].astype(jnp.float32), axis=0)).astype(jnp.bfloat16)
         far_copy = remote(far_out, far_in, far_send, far_recv.at[0], peer(0, across))
         far_copy.start()
 
@@ -497,9 +487,8 @@
             vmem((edges, attr_width), bf16),
             vmem((half, feat), bf16),
             vmem((half, feat), bf16),
-            vmem((half, feat), f32),
+            vmem((2, slab, feat), f32),
             vmem((slab, feat), f32),
-            vmem((rows, feat), f32),
             vmem((max(n_x - 2, 1), slab, feat), bf16),
             vmem((max(n_x - 2, 1), slab, feat), bf16),
             vmem((n_z - 1, rows, feat), bf16),

time: 40.3 us -> 40.3 us (level)
  no operation moved by 1% of the time
where the time goes in v5:
time: 40.3 us; the launch traced here: 40.2 us
  Pallas kernels  39.5 us (98%)
  between operations  0.64 us (2%)
    pallas_call x1, Pallas kernels, local(): pl.pallas_call(functools.partial(kernel, (n_src, n_x, n_z, rows)), out_sh...  38.7 us

profile of v5, /device:TPU:1, one launch (start us, length us, event | category | flops | bytes accessed | tf_op | source)
XLA Modules:
  0.0 40.2 jit_solution(16344469265157835142)
XLA Ops:
  0.6 38.7 %shard_map.130 = (bf16[16,256]{1,0:T(8,128)(2,1)S(1)}, bf16[16,256]{1,0:T(8,128)(2,1)S(1)}, bf16[1536,128]{1,0:T(8,128)(2,1)S(1)}) custom-call(bf16[16,256]{1,0:T(8,128)(2,1)} %feats_in.1, bf16[16,256]{1,0:T(8,128)(2,1)} %cot_in.1, bf16[1536,128]{1,0:T(8,128)(2,1)} %attr_in.1, s32[12,128]{1,0:T(8,128)} %bitcast.3, s32[12,128]{1,0:T(8,128)} %bitcast.4, ...), custom_call_target="tpu_custom_call" | custom-call | tf_op jit(solution)/shard_map/pallas_call | solution.py:462
  39.4 0.8 %shard_map.131 = (bf16[16,256]{1,0:T(8,128)(2,1)}, bf16[16,256]{1,0:T(8,128)(2,1)}, bf16[1536,128]{1,0:T(8,128)(2,1)}) custom-call(bf16[16,256]{1,0:T(8,128)(2,1)S(1)} %get-tuple-element.6.refs_0_, bf16[16,256]{1,0:T(8,128)(2,1)S(1)} %get-tuple-element.7.refs_1_, bf16[1536,128]{1,0:T(8,128)(2,1)S(1)} %get-tuple-element.8.refs_2_), custom_call_target="tpu_custom_call" | custom-call | tf_op jit(solution)/shard_map/pallas_call | solution.py:515

commit v6 on v5

--- a/solution.py
+++ b/solution.py
@@ -150,7 +150,7 @@
             hot_win[here, 0:width] = 0.5 * hot(inside == lane)
             hot_win[here, width : 2 * width] = 0.5 * hot(inside == lane + width)
 
-        loop(0, blocks // 4, mark)
+        mark(0)
 
     with jax.named_scope("barrier"):
         loads[4].wait()
@@ -192,7 +192,7 @@
             to_sibling(j, 1)
 
     with jax.named_scope("marks"):
-        loop(blocks // 4, blocks, mark)
+        loop(1, blocks, mark)
 
     with jax.named_scope("attr_part"):
         for i in (6, 7, 8):

time: 40.3 us -> 40.3 us (level)
  no operation moved by 1% of the time
where the time goes in v6:
time: 40.3 us; the launch traced here: 40.2 us
  Pallas kernels  39.5 us (98%)
  between operations  0.64 us (2%)
    pallas_call x1, Pallas kernels, local(): pl.pallas_call(functools.partial(kernel, (n_src, n_x, n_z, rows)), out_sh...  38.7 us

profile of v6, /device:TPU:1, one launch (start us, length us, event | category | flops | bytes accessed | tf_op | source)
XLA Modules:
  0.0 40.2 jit_solution(11936544640215442371)
XLA Ops:
  0.6 38.7 %shard_map.130 = (bf16[16,256]{1,0:T(8,128)(2,1)S(1)}, bf16[16,256]{1,0:T(8,128)(2,1)S(1)}, bf16[1536,128]{1,0:T(8,128)(2,1)S(1)}) custom-call(bf16[16,256]{1,0:T(8,128)(2,1)} %feats_in.1, bf16[16,256]{1,0:T(8,128)(2,1)} %cot_in.1, bf16[1536,128]{1,0:T(8,128)(2,1)} %attr_in.1, s32[12,128]{1,0:T(8,128)} %bitcast.3, s32[12,128]{1,0:T(8,128)} %bitcast.4, ...), custom_call_target="tpu_custom_call" | custom-call | tf_op jit(solution)/shard_map/pallas_call | solution.py:462
  39.4 0.8 %shard_map.131 = (bf16[16,256]{1,0:T(8,128)(2,1)}, bf16[16,256]{1,0:T(8,128)(2,1)}, bf16[1536,128]{1,0:T(8,128)(2,1)}) custom-call(bf16[16,256]{1,0:T(8,128)(2,1)S(1)} %get-tuple-element.6.refs_0_, bf16[16,256]{1,0:T(8,128)(2,1)S(1)} %get-tuple-element.7.refs_1_, bf16[1536,128]{1,0:T(8,128)(2,1)S(1)} %get-tuple-element.8.refs_2_), custom_call_target="tpu_custom_call" | custom-call | tf_op jit(solution)/shard_map/pallas_call | solution.py:515
